TPU v7x, 32 devices: a whole 2x2x4 slice. The times are simulated.
32 devices in a mesh: wide: 8 (over z, x), gy: 4 (over y, core).
Axes of the slice: x: 2, y: 2, z: 4, core: 2. Of those that a mesh axis runs over, the one named last changes fastest.
Arguments:
- omega: bfloat16 [64, 512, 1024], P(None, 'wide', 'gy'), may hold values from -6 to 6
- coefficients: float32 [4, 512, 1024], P(None, 'wide', 'gy'), may hold values from -0.75 to 3.6, as said below
- obs_rows: bfloat16 [64, 102400], P(None, ('wide', 'gy')), may hold values from -6 to 6
- obs_cell: int32 [102400], P(('wide', 'gy')), may hold values from 0 to 16383
- obs_count: int32 [32, 32], P(('wide', 'gy')), may hold values from 0 to 128, as said below
Outputs:
- applied: bfloat16 [64, 512, 1024], P(None, 'wide', 'gy')
- gram: float32 [64, 64], replicated
- data_field: bfloat16 [64, 512, 1024], P(None, 'wide', 'gy')
Inputs may be any that keep to these rules, and one draw needn't show every extreme that they name: `coefficients`: kappa squared lies in [0.05, 3], the row and column conductivities in [0.3, 3.6], the cross conductivity in [-0.75, 0.75]. `obs_count`: each row sums to at most 3200; some entry equals 128 in every draw, and some owner gets 128 rows from every block.
All inputs are finite; a program needn't handle non-finite values.
Results may differ from a plain program's by a relative error of at most 0.0043.
Values may be sent and summed in bfloat16 or wider, within the bound.
A program may use at most 128 MiB of HBM per device.

v0:
```python
import jax
import jax.numpy as jnp
from jax import lax
from jax.sharding import PartitionSpec as P

CAP = 128


def with_halo(block, sides, width):
    for axis, dim in sides:
        count = lax.axis_size(axis)
        forward = [(i, i + 1) for i in range(count - 1)]
        backward = [(target, source) for source, target in forward]
        low = lax.ppermute(
            lax.slice_in_dim(block, block.shape[dim] - width, None, axis=dim), axis, forward
        )
        high = lax.ppermute(lax.slice_in_dim(block, 0, width, axis=dim), axis, backward)
        block = jnp.concatenate([low, block, high], axis=dim)
    return block


def operator_apply(field, coef):
    kappa_sq = coef[0]
    cond_rows = coef[1]
    cond_cols = coef[2]
    cond_cross = coef[3]
    centre = field[..., 1:-1, 1:-1]
    face_south = 0.5 * (cond_rows[1:-1, 1:-1] + cond_rows[2:, 1:-1])
    face_north = 0.5 * (cond_rows[1:-1, 1:-1] + cond_rows[:-2, 1:-1])
    face_east = 0.5 * (cond_cols[1:-1, 1:-1] + cond_cols[1:-1, 2:])
    face_west = 0.5 * (cond_cols[1:-1, 1:-1] + cond_cols[1:-1, :-2])
    diffusion = face_south * (field[..., 2:, 1:-1] - centre) - face_north * (
        centre - field[..., :-2, 1:-1]
    )
    diffusion = (
        diffusion
        + face_east * (field[..., 1:-1, 2:] - centre)
        - face_west * (centre - field[..., 1:-1, :-2])
    )
    mixed = cond_cross[2:, 1:-1] * (field[..., 2:, 2:] - field[..., 2:, :-2]) - cond_cross[
        :-2, 1:-1
    ] * (field[..., :-2, 2:] - field[..., :-2, :-2])
    mixed = (
        mixed
        + cond_cross[1:-1, 2:] * (field[..., 2:, 2:] - field[..., :-2, 2:])
        - cond_cross[1:-1, :-2] * (field[..., 2:, :-2] - field[..., :-2, :-2])
    )
    return kappa_sq[1:-1, 1:-1] * centre - diffusion - 0.25 * mixed


def per_device(omega, coefficients, obs_rows, obs_cell, obs_count):
    columns, tile_rows, tile_cols = omega.shape
    wide_count = lax.axis_size("wide")
    gy_count = lax.axis_size("gy")
    devices_all = wide_count * gy_count
    coef_pad = with_halo(coefficients, (("wide", 1), ("gy", 2)), 1)
    sketch_pad = with_halo(omega, (("wide", 1), ("gy", 2)), 1)
    image = operator_apply(sketch_pad.astype(jnp.float32), coef_pad).astype(jnp.bfloat16)
    image = lax.optimization_barrier(image)
    image_pad = with_halo(image, (("wide", 1), ("gy", 2)), 1)
    second = operator_apply(image_pad.astype(jnp.float32), coef_pad)
    applied = (0.0625 * second).astype(jnp.bfloat16)
    local_gram = lax.dot_general(
        omega.reshape(columns, tile_rows * tile_cols),
        applied.reshape(columns, tile_rows * tile_cols),
        (((1,), (1,)), ((), ())),
        preferred_element_type=jnp.float32,
    )
    summed = lax.psum(local_gram, ("wide", "gy"))
    gram = summed / (tile_rows * tile_cols * devices_all)
    counts_row = obs_count[0]
    ends = jnp.cumsum(counts_row)
    starts = ends - counts_row
    padded_rows = jnp.pad(obs_rows, ((0, 0), (0, CAP)))
    padded_cells = jnp.pad(obs_cell, (0, CAP))
    slot_index = jnp.arange(CAP, dtype=jnp.int32)
    positions = starts[:, None] + slot_index[None, :]
    rows_win = jnp.transpose(jnp.take(padded_rows, positions, axis=1), (1, 0, 2))
    cells_win = padded_cells[positions][:, None, :]
    valid = (slot_index[None, :] < counts_row[:, None])[:, None, :]
    send_rows = jnp.where(valid, rows_win, jnp.zeros((), jnp.bfloat16))
    send_cells = jnp.where(valid, cells_win, tile_rows * tile_cols)
    got_rows, got_cells = (
        lax.all_to_all(send_rows, ("wide", "gy"), split_axis=0, concat_axis=0, tiled=True),
        lax.all_to_all(send_cells, ("wide", "gy"), split_axis=0, concat_axis=0, tiled=True),
    )
    flat_rows = jnp.transpose(got_rows, (1, 0, 2)).reshape(columns, devices_all * CAP)
    flat_cells = got_cells.reshape(devices_all * CAP)
    binned = (
        jnp.zeros((columns, tile_rows * tile_cols), jnp.float32)
        .at[:, flat_cells]
        .add(flat_rows.astype(jnp.float32), mode="drop")
    )
    data_field = binned.astype(jnp.bfloat16).reshape(columns, tile_rows, tile_cols)
    return (applied, gram, data_field)


def solution(mesh):
    in_specs = (
        P(None, "wide", "gy"),
        P(None, "wide", "gy"),
        P(None, ("wide", "gy")),
        P(("wide", "gy")),
        P(("wide", "gy"), None),
    )
    out_specs = (P(None, "wide", "gy"), P(), P(None, "wide", "gy"))
    return jax.shard_map(
        per_device, mesh=mesh, in_specs=in_specs, out_specs=out_specs, check_vma=False
    )
```

profile of v0, /device:TPU:0, one launch (start us, length us, event | category | flops | bytes accessed | tf_op | source)
XLA Modules:
  0.0 308.1 jit_solution(12874671670048970189)
XLA Ops:
  0.6 0.8 fusion.36
  1.4 4.8 %collective-permute-start = (f32[4,1,256]{2,1,0:T(1,128)S(1)}, f32[4,1,256]{2,1,0:T(1,128)S(1)}, u32[]{:S(2)}, u32[]{:S(2)}) collective-permute-start(f32[4,1,256]{2,1,0:T(1,128)S(1)} %get-tuple-element.32), channel_id=1, source_target_pairs={{0,4},{4,8},{8,12},{12,16},{16,20},{20,24},{24,28},{1,5},{5,9},{9,... | collective-permute-start | bytes 12296 | tf_op jit(solution)/shard_map/ppermute | solution.py:14
  6.3 1.3 collective-permute-start.1
  7.6 1.1 fusion.34
  8.7 0.6 copy.95
  9.3 5.1 %collective-permute-start.4 = (bf16[64,1,256]{2,0,1:T(8,128)(2,1)}, bf16[64,1,256]{2,0,1:T(8,128)(2,1)}, u32[]{:S(2)}, u32[]{:S(2)}) collective-permute-start(bf16[64,1,256]{2,0,1:T(8,128)(2,1)} %copy.95), channel_id=1, source_target_pairs={{0,4},{4,8},{8,12},{12,16},{16,20},{20,24},{24,28},{1,5},{5,9},{9,... | collective-permute-start | bytes 98312 | tf_op jit(solution)/shard_map/ppermute | solution.py:14
  14.5 0.6 copy.94
  15.1 1.3 collective-permute-start.5
  16.4 0.7 copy.82
  17.2 0.1 reduce
  17.3 0.7 bitcast_subtract_fusion
  18.0 0.7 pad.8
  18.8 23.0 %gather_fusion = s32[4096]{0:T(1024)S(1)} fusion(s32[3328]{0:T(1024)S(1)} %pad.8, s32[4096]{0:T(1024)S(1)} %fusion.28), kind=kCustom, calls=%fused_computation | custom fusion | bytes 49152 | tf_op jit(solution)/shard_map/gather | solution.py:79
  41.8 0.7 compare_select_fusion.1
  42.5 7.3 %all-to-all-start = ((s32[32,1,128]{2,1,0:T(1,128)}), s32[32,1,128]{2,1,0:T(1,128)S(1)}, u32[]{:S(2)}, u32[]{:S(2)}) async-start(s32[32,1,128]{2,1,0:T(1,128)} %compare_select_fusion.1), calls=%async_computation | async-start | bytes 32768 | tf_op jit(solution)/shard_map/all_to_all | solution.py:85
  49.9 0.8 fusion.35
  50.7 2.2 collective-permute-start.2
  52.8 1.3 collective-permute-start.3
  54.1 0.7 iota_compare_fusion
  54.8 6.6 %copy.66 = bf16[64,64,256]{1,0,2:T(8,128)(2,1)} copy(bf16[64,64,256]{2,1,0:T(8,128)(2,1)S(1)} %copy-done) | data formatting | bytes 4194304 | tf_op args[0]
  61.5 0.4 copy.83
  61.9 0.2 pad.9
  62.0 12.1 %gather_fusion.1 = bf16[4096,64]{1,0:T(8,128)(2,1)S(1)} fusion(bf16[64,3328]{0,1:T(8,128)(2,1)S(1)} %pad.9, s32[4096]{0:T(1024)S(1)} %fusion.28), kind=kCustom, calls=%fused_computation.1 | custom fusion | bytes 1064960 | tf_op jit(solution)/shard_map/jit(_take)/gather | solution.py:78
  74.2 0.4 copy.84
  74.6 0.9 pad_maximum_fusion
  75.6 0.2 fusion.24
  75.8 7.6 %copy.65 = bf16[64,1,256]{1,0,2:T(8,128)(2,1)} copy(bf16[64,1,256]{2,0,1:T(8,128)(2,1)} %collective-permute-done.4) | data formatting | bytes 65536 | tf_op jit(solution)/shard_map/ppermute | solution.py:14
  83.3 7.5 %copy.67 = bf16[64,1,256]{1,0,2:T(8,128)(2,1)} copy(bf16[64,1,256]{2,0,1:T(8,128)(2,1)} %collective-permute-done.5) | data formatting | bytes 65536 | tf_op jit(solution)/shard_map/ppermute | solution.py:17
  90.8 0.9 pad_maximum_fusion.7
  91.7 4.2 %collective-permute-start.6 = (bf16[64,66,1]{1,0,2:T(8,128)(2,1)S(1)}, bf16[64,66,1]{1,0,2:T(8,128)(2,1)S(1)}, u32[]{:S(2)}, u32[]{:S(2)}) collective-permute-start(bf16[64,66,1]{1,0,2:T(8,128)(2,1)S(1)} %get-tuple-element.20), channel_id=1, source_target_pairs={{0,1},{1,2},{2,3},{4,5},{5,6},{6,7},{8,9},{9,10},{10,11},{12,13},{... | collective-permute-start | bytes 25352 | tf_op jit(solution)/shard_map/ppermute | solution.py:14
  95.9 1.5 collective-permute-start.7
  97.4 0.1 fusion.37
  97.6 0.1 copy.69
  97.7 0.1 copy.70
  97.8 0.1 copy.71
  97.9 0.1 copy.72
  98.1 0.1 copy.74
  98.2 0.1 copy.75
  98.5 1.7 collective-permute-done.7
  100.2 6.6 %maximum_convert_fusion = f32[64,66,258]{1,0,2:T(8,128)S(1)} fusion(bf16[64,66,1]{1,0,2:T(8,128)(2,1)S(1)} %collective-permute-done.7, bf16[64,1,256]{1,0,2:T(8,128)(2,1)} %copy.67, bf16[64,64,256]{1,0,2:T(8,128)(2,1)} %copy.66, bf16[64,1,256]{1,0,2:T(8,128)(2,1)} %copy.65, bf16[64,66,1]{1,0,2:T(8,128)(2,1)S(1)} %collective-permute-done.6), kind=kLoop, calls=%fused_computation.32 | loop fusion | flops 10897920 | bytes 6538752 | tf_op jit(solution)/shard_map/convert_element_type | solution.py:58
  106.8 22.6 %fusion.15 = bf16[64,64,256]{1,0,2:T(8,128)(2,1)} fusion(f32[64,66,258]{1,0,2:T(8,128)S(1)} %maximum_convert_fusion, f32[64,256]{0,1:T(8,128)S(1)} %copy.75, f32[64,256]{0,1:T(8,128)S(1)} %copy.74, f32[64,256]{0,1:T(8,128)S(1)} %copy.73, f32[64,256]{0,1:T(8,128)S(1)} %copy.72, f32[64,256]{0,1:T(8,128)S(1)} %copy.71, f32[64,256]{0,1:T(8,128)S(1)} %copy.70, ...), kind=kLoop, calls=%fused_computation.23 | loop fusion | flops 28311552 | bytes 40435712 | tf_op jit(solution)/shard_map/convert_element_type | solution.py:58
  129.4 7.4 %fusion.33 = (bf16[64,1,256]{1,0,2:T(8,128)(2,1)}, bf16[64,1,256]{1,0,2:T(8,128)(2,1)}) fusion(bf16[64,64,256]{1,0,2:T(8,128)(2,1)} %fusion.15), kind=kLoop, calls=%fused_computation.73 | loop fusion | bytes 131072 | tf_op jit(solution)/shard_map/slice | solution.py:15
  136.9 5.6 %copy.76 = bf16[64,1,256]{2,0,1:T(8,128)(2,1)S(1)} copy(bf16[64,1,256]{1,0,2:T(8,128)(2,1)} %get-tuple-element.22) | data formatting | bytes 65536 | tf_op jit(solution)/shard_map/slice | solution.py:15
  142.5 3.4 %collective-permute-start.8 = (bf16[64,1,256]{2,0,1:T(8,128)(2,1)S(1)}, bf16[64,1,256]{2,0,1:T(8,128)(2,1)S(1)}, u32[]{:S(2)}, u32[]{:S(2)}) collective-permute-start(bf16[64,1,256]{2,0,1:T(8,128)(2,1)S(1)} %copy.76), channel_id=1, source_target_pairs={{0,4},{4,8},{8,12},{12,16},{16,20},{20,24},{24,28},{1,5},{5,9},{9,... | collective-permute-start | bytes 98312 | tf_op jit(solution)/shard_map/ppermute | solution.py:14
  145.8 5.6 %copy.77 = bf16[64,1,256]{2,0,1:T(8,128)(2,1)S(1)} copy(bf16[64,1,256]{1,0,2:T(8,128)(2,1)} %get-tuple-element.23) | data formatting | bytes 65536 | tf_op jit(solution)/shard_map/slice | solution.py:17
  151.5 1.3 collective-permute-start.9
  152.8 0.9 select_bitcast_fusion
  153.7 6.8 %copy.78 = bf16[64,1,256]{1,0,2:T(8,128)(2,1)} copy(bf16[64,1,256]{2,0,1:T(8,128)(2,1)S(1)} %collective-permute-done.8) | data formatting | bytes 65536 | tf_op jit(solution)/shard_map/ppermute | solution.py:14
  160.5 6.9 %copy.79 = bf16[64,1,256]{1,0,2:T(8,128)(2,1)} copy(bf16[64,1,256]{2,0,1:T(8,128)(2,1)S(1)} %collective-permute-done.9) | data formatting | bytes 65536 | tf_op jit(solution)/shard_map/ppermute | solution.py:17
  167.4 0.9 pad_maximum_fusion.4
  168.3 4.1 %collective-permute-start.10 = (bf16[64,66,1]{1,0,2:T(8,128)(2,1)S(1)}, bf16[64,66,1]{1,0,2:T(8,128)(2,1)S(1)}, u32[]{:S(2)}, u32[]{:S(2)}) collective-permute-start(bf16[64,66,1]{1,0,2:T(8,128)(2,1)S(1)} %get-tuple-element.18), channel_id=1, source_target_pairs={{0,1},{1,2},{2,3},{4,5},{5,6},{6,7},{8,9},{9,10},{10,11},{12,13},{... | collective-permute-start | bytes 25352 | tf_op jit(solution)/shard_map/ppermute | solution.py:14
  172.4 1.3 collective-permute-start.11
  173.7 8.0 %all-to-all-start.1 = ((bf16[32,64,128]{2,1,0:T(8,128)(2,1)}), bf16[32,64,128]{2,1,0:T(8,128)(2,1)S(1)}, u32[]{:S(2)}, u32[]{:S(2)}) async-start(bf16[32,64,128]{2,1,0:T(8,128)(2,1)} %select_bitcast_fusion), calls=%async_computation.1 | async-start | bytes 1048576 | tf_op jit(solution)/shard_map/all_to_all | solution.py:84
  181.8 6.6 %maximum_convert_fusion.1 = f32[64,66,258]{1,0,2:T(8,128)S(1)} fusion(bf16[64,66,1]{1,0,2:T(8,128)(2,1)S(1)} %collective-permute-done.11, bf16[64,1,256]{1,0,2:T(8,128)(2,1)} %copy.79, bf16[64,64,256]{1,0,2:T(8,128)(2,1)} %fusion.15, bf16[64,1,256]{1,0,2:T(8,128)(2,1)} %copy.78, bf16[64,66,1]{1,0,2:T(8,128)(2,1)S(1)} %collective-permute-done.10), kind=kLoop, calls=%fused_computation.33 | loop fusion | flops 10897920 | bytes 6538752 | tf_op jit(solution)/shard_map/convert_element_type | solution.py:61
  188.4 22.8 %fusion.5 = bf16[64,64,256]{1,0,2:T(8,128)(2,1)} fusion(f32[64,66,258]{1,0,2:T(8,128)S(1)} %maximum_convert_fusion.1, f32[64,256]{0,1:T(8,128)S(1)} %copy.75, f32[64,256]{0,1:T(8,128)S(1)} %copy.74, f32[64,256]{0,1:T(8,128)S(1)} %copy.73, f32[64,256]{0,1:T(8,128)S(1)} %copy.72, f32[64,256]{0,1:T(8,128)S(1)} %copy.71, f32[64,256]{0,1:T(8,128)S(1)} %copy.70, ...), kind=kLoop, calls=%fused_computation.9 | loop fusion | flops 29360128 | bytes 40435712 | tf_op jit(solution)/shard_map/convert_element_type | solution.py:62
  211.3 7.9 %copy.80 = bf16[64,64,256]{2,0,1:T(8,128)(2,1)} copy(bf16[64,64,256]{1,0,2:T(8,128)(2,1)} %fusion.5) | data formatting | bytes 4194304 | tf_op jit(solution)/shard_map/convert_element_type | solution.py:62
  219.2 5.9 %copy.87 = bf16[64,64,256]{2,1,0:T(8,128)(2,1)} copy(bf16[64,64,256]{1,0,2:T(8,128)(2,1)} %fusion.5) | data formatting | bytes 4194304
  225.1 4.0 %convolution_bitcast_fusion = f32[64,64]{0,1:T(8,128)S(1)} fusion(bf16[64,64,256]{2,0,1:T(8,128)(2,1)} %copy.80, bf16[64,64,256]{2,1,0:T(8,128)(2,1)S(1)} %copy-done.1), kind=kOutput, calls=%fused_computation.36 | convolution fusion | flops 134217728 | bytes 4210688 | tf_op jit(solution)/shard_map/dot_general | solution.py:63
  229.1 40.7 %psum.7 = f32[64,64]{0,1:T(8,128)S(1)} all-reduce(f32[64,64]{0,1:T(8,128)S(1)} %convolution_bitcast_fusion), channel_id=1, replica_groups=mesh['wide'=8,'gy'=4] {'wide','gy'}, use_global_device_ids=true, to_apply=%region_0.0 | all-reduce | flops 4096 | bytes 32768 | tf_op jit(solution)/shard_map/psum | solution.py:69
  269.8 0.7 copy.88
  270.6 0.6 copy.86
  271.2 26.1 %scatter_custom_fusion = f32[64,16384]{0,1:T(8,128)} fusion(s32[4096]{0:T(1024)S(1)} %bitcast.39, f32[4096,64]{1,0:T(8,128)S(1)} %copy.86, f32[]{:T(128)} %constant.15.clone.1), kind=kCustom, calls=%fused_computation.34 | custom fusion | flops 262144 | bytes 4194308 | tf_op jit(solution)/shard_map/scatter-add | solution.py:92
  297.3 5.1 %convert_element_type.33 = bf16[64,16384]{0,1:T(8,128)(2,1)} convert(f32[64,16384]{0,1:T(8,128)} %scatter_custom_fusion) | non-fusion elementwise | flops 1048576 | bytes 6291456 | tf_op jit(solution)/shard_map/convert_element_type | solution.py:94
  302.4 5.6 %copy.89 = bf16[64,64,256]{2,1,0:T(8,128)(2,1)} copy(bf16[64,64,256]{0,2,1:T(8,128)(2,1)} %bitcast.36) | data formatting | bytes 4194304
  (42 shorter events, 0.7 us)
Async XLA Ops:
  1.4 48.4 %collective-permute-start = (f32[4,1,256]{2,1,0:T(1,128)S(1)}, f32[4,1,256]{2,1,0:T(1,128)S(1)}, u32[]{:S(2)}, u32[]{:S(2)}) collective-permute-start(f32[4,1,256]{2,1,0:T(1,128)S(1)} %get-tuple-element.32), channel_id=1, source_target_pairs={{0,4},{4,8},{8,12},{12,16},{16,20},{20,24},{24,28},{1,5},{5,9},{9,... | collective-permute-start | bytes 12296 | tf_op jit(solution)/shard_map/ppermute | solution.py:14
  6.3 43.6 %collective-permute-start.1 = (f32[4,1,256]{2,1,0:T(1,128)S(1)}, f32[4,1,256]{2,1,0:T(1,128)S(1)}, u32[]{:S(2)}, u32[]{:S(2)}) collective-permute-start(f32[4,1,256]{2,1,0:T(1,128)S(1)} %get-tuple-element.33), channel_id=1, source_target_pairs={{4,0},{8,4},{12,8},{16,12},{20,16},{24,20},{28,24},{5,1},{9,5},{13... | collective-permute-start | bytes 12296 | tf_op jit(solution)/shard_map/ppermute | solution.py:17
  9.3 66.4 %collective-permute-start.4 = (bf16[64,1,256]{2,0,1:T(8,128)(2,1)}, bf16[64,1,256]{2,0,1:T(8,128)(2,1)}, u32[]{:S(2)}, u32[]{:S(2)}) collective-permute-start(bf16[64,1,256]{2,0,1:T(8,128)(2,1)} %copy.95), channel_id=1, source_target_pairs={{0,4},{4,8},{8,12},{12,16},{16,20},{20,24},{24,28},{1,5},{5,9},{9,... | collective-permute-start | bytes 98312 | tf_op jit(solution)/shard_map/ppermute | solution.py:14
  15.1 68.3 %collective-permute-start.5 = (bf16[64,1,256]{2,0,1:T(8,128)(2,1)}, bf16[64,1,256]{2,0,1:T(8,128)(2,1)}, u32[]{:S(2)}, u32[]{:S(2)}) collective-permute-start(bf16[64,1,256]{2,0,1:T(8,128)(2,1)} %copy.94), channel_id=1, source_target_pairs={{4,0},{8,4},{12,8},{16,12},{20,16},{24,20},{28,24},{5,1},{9,5},{13... | collective-permute-start | bytes 98312 | tf_op jit(solution)/shard_map/ppermute | solution.py:17
  18.7 23.1 %copy-start.8 = (s32[1,32]{1,0:T(1,128)S(1)}, s32[1,32]{1,0:T(1,128)}, u32[]{:S(2)}) copy-start(s32[1,32]{1,0:T(1,128)} %param.9) | copy-start | bytes 388
  18.7 31.1 %copy-start.2 = (f32[4,64,256]{2,1,0:T(8,128)S(1)}, f32[4,64,256]{2,1,0:T(8,128)}, u32[]{:S(2)}) copy-start(f32[4,64,256]{2,1,0:T(8,128)} %param.6) | copy-start | bytes 786436
  18.7 36.1 %copy-start = (bf16[64,64,256]{2,1,0:T(8,128)(2,1)S(1)}, bf16[64,64,256]{2,1,0:T(8,128)(2,1)}, u32[]{:S(2)}) copy-start(bf16[64,64,256]{2,1,0:T(8,128)(2,1)} %param.5) | copy-start | bytes 6291460
  18.7 42.7 %copy-start.3 = (bf16[64,3200]{1,0:T(8,128)(2,1)S(1)}, bf16[64,3200]{1,0:T(8,128)(2,1)}, u32[]{:S(2)}) copy-start(bf16[64,3200]{1,0:T(8,128)(2,1)} %param.7) | copy-start | bytes 1228804
  42.5 131.2 %all-to-all-start = ((s32[32,1,128]{2,1,0:T(1,128)}), s32[32,1,128]{2,1,0:T(1,128)S(1)}, u32[]{:S(2)}, u32[]{:S(2)}) async-start(s32[32,1,128]{2,1,0:T(1,128)} %compare_select_fusion.1), calls=%async_computation | async-start | bytes 32768 | tf_op jit(solution)/shard_map/all_to_all | solution.py:85
  49.8 24.4 %copy-start.4 = (f32[4,1,256]{2,1,0:T(1,128)}, f32[4,1,256]{2,1,0:T(1,128)S(1)}, u32[]{:S(2)}) copy-start(f32[4,1,256]{2,1,0:T(1,128)S(1)} %collective-permute-done) | copy-start | bytes 12292
  49.9 24.3 %copy-start.5 = (f32[4,1,256]{2,1,0:T(1,128)}, f32[4,1,256]{2,1,0:T(1,128)S(1)}, u32[]{:S(2)}) copy-start(f32[4,1,256]{2,1,0:T(1,128)S(1)} %collective-permute-done.1) | copy-start | bytes 12292
  50.7 23.9 %collective-permute-start.2 = (f32[4,66,1]{2,1,0:T(8,128)}, f32[4,66,1]{2,1,0:T(8,128)S(1)}, u32[]{:S(2)}, u32[]{:S(2)}) collective-permute-start(f32[4,66,1]{2,1,0:T(8,128)} %get-tuple-element.30), channel_id=1, source_target_pairs={{0,1},{1,2},{2,3},{4,5},{5,6},{6,7},{8,9},{9,10},{10,11},{12,13},{... | collective-permute-start | bytes 3176 | tf_op jit(solution)/shard_map/ppermute | solution.py:14
  52.8 21.8 %collective-permute-start.3 = (f32[4,66,1]{2,1,0:T(8,128)S(1)}, f32[4,66,1]{2,1,0:T(8,128)S(1)}, u32[]{:S(2)}, u32[]{:S(2)}) collective-permute-start(f32[4,66,1]{2,1,0:T(8,128)S(1)} %get-tuple-element.31), channel_id=1, source_target_pairs={{1,0},{2,1},{3,2},{5,4},{6,5},{7,6},{9,8},{10,9},{11,10},{13,12},{... | collective-permute-start | bytes 3176 | tf_op jit(solution)/shard_map/ppermute | solution.py:17
  91.7 6.8 %collective-permute-start.6 = (bf16[64,66,1]{1,0,2:T(8,128)(2,1)S(1)}, bf16[64,66,1]{1,0,2:T(8,128)(2,1)S(1)}, u32[]{:S(2)}, u32[]{:S(2)}) collective-permute-start(bf16[64,66,1]{1,0,2:T(8,128)(2,1)S(1)} %get-tuple-element.20), channel_id=1, source_target_pairs={{0,1},{1,2},{2,3},{4,5},{5,6},{6,7},{8,9},{9,10},{10,11},{12,13},{... | collective-permute-start | bytes 25352 | tf_op jit(solution)/shard_map/ppermute | solution.py:14
  95.9 4.3 %collective-permute-start.7 = (bf16[64,66,1]{1,0,2:T(8,128)(2,1)S(1)}, bf16[64,66,1]{1,0,2:T(8,128)(2,1)S(1)}, u32[]{:S(2)}, u32[]{:S(2)}) collective-permute-start(bf16[64,66,1]{1,0,2:T(8,128)(2,1)S(1)} %get-tuple-element.21), channel_id=1, source_target_pairs={{1,0},{2,1},{3,2},{5,4},{6,5},{7,6},{9,8},{10,9},{11,10},{13,12},{... | collective-permute-start | bytes 25352 | tf_op jit(solution)/shard_map/ppermute | solution.py:17
  136.9 15.9 %copy-start.6 = (pred[32,128]{1,0:T(8,128)(4,1)S(1)}, pred[32,128]{1,0:T(8,128)(4,1)}, u32[]{:S(2)}) copy-start(pred[32,128]{1,0:T(8,128)(4,1)} %get-tuple-element.44) | copy-start | bytes 12292
  136.9 15.9 %copy-start.7 = (pred[32,128]{1,0:T(8,128)(4,1)S(1)}, pred[32,128]{1,0:T(8,128)(4,1)}, u32[]{:S(2)}) copy-start(pred[32,128]{1,0:T(8,128)(4,1)} %get-tuple-element.45) | copy-start | bytes 12292
  142.5 11.3 %collective-permute-start.8 = (bf16[64,1,256]{2,0,1:T(8,128)(2,1)S(1)}, bf16[64,1,256]{2,0,1:T(8,128)(2,1)S(1)}, u32[]{:S(2)}, u32[]{:S(2)}) collective-permute-start(bf16[64,1,256]{2,0,1:T(8,128)(2,1)S(1)} %copy.76), channel_id=1, source_target_pairs={{0,4},{4,8},{8,12},{12,16},{16,20},{20,24},{24,28},{1,5},{5,9},{9,... | collective-permute-start | bytes 98312 | tf_op jit(solution)/shard_map/ppermute | solution.py:14
  151.5 9.1 %collective-permute-start.9 = (bf16[64,1,256]{2,0,1:T(8,128)(2,1)S(1)}, bf16[64,1,256]{2,0,1:T(8,128)(2,1)S(1)}, u32[]{:S(2)}, u32[]{:S(2)}) collective-permute-start(bf16[64,1,256]{2,0,1:T(8,128)(2,1)S(1)} %copy.77), channel_id=1, source_target_pairs={{4,0},{8,4},{12,8},{16,12},{20,16},{24,20},{28,24},{5,1},{9,5},{13... | collective-permute-start | bytes 98312 | tf_op jit(solution)/shard_map/ppermute | solution.py:17
  168.3 13.5 %collective-permute-start.10 = (bf16[64,66,1]{1,0,2:T(8,128)(2,1)S(1)}, bf16[64,66,1]{1,0,2:T(8,128)(2,1)S(1)}, u32[]{:S(2)}, u32[]{:S(2)}) collective-permute-start(bf16[64,66,1]{1,0,2:T(8,128)(2,1)S(1)} %get-tuple-element.18), channel_id=1, source_target_pairs={{0,1},{1,2},{2,3},{4,5},{5,6},{6,7},{8,9},{9,10},{10,11},{12,13},{... | collective-permute-start | bytes 25352 | tf_op jit(solution)/shard_map/ppermute | solution.py:14
  172.4 9.4 %collective-permute-start.11 = (bf16[64,66,1]{1,0,2:T(8,128)(2,1)S(1)}, bf16[64,66,1]{1,0,2:T(8,128)(2,1)S(1)}, u32[]{:S(2)}, u32[]{:S(2)}) collective-permute-start(bf16[64,66,1]{1,0,2:T(8,128)(2,1)S(1)} %get-tuple-element.19), channel_id=1, source_target_pairs={{1,0},{2,1},{3,2},{5,4},{6,5},{7,6},{9,8},{10,9},{11,10},{13,12},{... | collective-permute-start | bytes 25352 | tf_op jit(solution)/shard_map/ppermute | solution.py:17
  173.7 96.8 %all-to-all-start.1 = ((bf16[32,64,128]{2,1,0:T(8,128)(2,1)}), bf16[32,64,128]{2,1,0:T(8,128)(2,1)S(1)}, u32[]{:S(2)}, u32[]{:S(2)}) async-start(bf16[32,64,128]{2,1,0:T(8,128)(2,1)} %select_bitcast_fusion), calls=%async_computation.1 | async-start | bytes 1048576 | tf_op jit(solution)/shard_map/all_to_all | solution.py:84
  211.3 13.8 %copy-start.1 = (bf16[64,64,256]{2,1,0:T(8,128)(2,1)S(1)}, bf16[64,64,256]{2,1,0:T(8,128)(2,1)}, u32[]{:S(2)}) copy-start(bf16[64,64,256]{2,1,0:T(8,128)(2,1)} %param.5) | copy-start | bytes 6291460
where the time goes:
time: 309 us; the launch traced here: 308 us
  local copies, waits for them, and re-layouts  117 us (38%)
  other arithmetic  96.1 us (31%)
  starting transfers between devices  47 us (15%)
  blocking collectives  40.7 us (13%)
  matrix products  4.04 us (1%)
    psum x1, blocking collectives, per_device(): summed = lax.psum(local_gram, ('wide', 'gy'))  40.7 us
    scatter-add x1, other arithmetic, per_device(): binned = jnp.zeros((columns, tile_rows * tile_cols), jnp.float32).at[:, f...  26.1 us
    ppermute x6, starting transfers between devices, with_halo(): lax.ppermute(lax.slice_in_dim(block, block.shape[dim] - width, None, axis...  23.7 us
    gather x1, local copies, waits for them, and re-layouts, per_device(): cells_win = padded_cells[positions][:, None, :]  23 us
    convert_element_type x1, other arithmetic, per_device(): applied = (0.0625 * second).astype(jnp.bfloat16)  22.8 us
    convert_element_type x1, other arithmetic, per_device(): operator_apply(sketch_pad.astype(jnp.float32), coef_pad)  22.6 us
    unnamed x25, local copies, waits for them, and re-layouts  20.5 us
    slice x5, local copies, waits for them, and re-layouts, with_halo(): lax.slice_in_dim(block, block.shape[dim] - width, None, axis=dim)  15.7 us
  transfers between devices with their start and end apart: 14, of which 1 were waited for; matrix products, arithmetic and copies ran while one was open for 58% of the time, Pallas kernels for 0%

commit v1 on v0

--- a/solution.py
+++ b/solution.py
@@ -1,6 +1,8 @@
 import jax
 import jax.numpy as jnp
 from jax import lax
+from jax.experimental import pallas as pl
+from jax.experimental.pallas import tpu as pltpu
 from jax.sharding import PartitionSpec as P
 
 CAP = 128
@@ -48,6 +50,111 @@
     return kappa_sq[1:-1, 1:-1] * centre - diffusion - 0.25 * mixed
 
 
+def pack_kernel(counts_ref, rows_ref, cells_ref, out_ref):
+    owners, _, _ = out_ref.shape
+    columns, length = rows_ref.shape
+    window = 2 * CAP
+    tile_cols = 256
+    slot = lax.broadcasted_iota(jnp.int32, (1, CAP), 1)
+    sub = lax.broadcasted_iota(jnp.int32, (16, CAP), 0)
+
+    def body(o, start):
+        count = counts_ref[o]
+        base = jnp.minimum((start // CAP) * CAP, length - window)
+        base = pl.multiple_of(base, CAP)
+        shift = lax.rem(2 * window - (start - base), window)
+        rows = rows_ref[:, pl.ds(base, window)].astype(jnp.float32)
+        rows = pltpu.roll(rows, shift, 1)[:, :CAP]
+        used = slot < count
+        out_ref[o, 0:columns, :] = jnp.where(used, rows, 0.0).astype(jnp.bfloat16)
+        cells = jnp.broadcast_to(cells_ref[:, pl.ds(base, window)], (8, window))
+        cells = pltpu.roll(cells, shift, 1)[0:1, :CAP]
+        cell_row = jnp.where(used, cells // tile_cols, 128)
+        cell_col = jnp.where(used, cells % tile_cols, 0)
+        both = jnp.where(sub == 0, cell_row, jnp.where(sub == 1, cell_col, 0))
+        out_ref[o, columns : columns + 16, :] = both.astype(jnp.float32).astype(jnp.bfloat16)
+        return start + count
+
+    lax.fori_loop(0, owners, body, jnp.int32(0))
+
+
+def pack_windows(counts, rows, cells):
+    columns = rows.shape[0]
+    owners = counts.shape[0]
+    smem = pl.BlockSpec(memory_space=pltpu.SMEM)
+    vmem = pl.BlockSpec(memory_space=pltpu.VMEM)
+    return pl.pallas_call(
+        pack_kernel,
+        out_shape=jax.ShapeDtypeStruct((owners, columns + 16, CAP), jnp.bfloat16),
+        in_specs=[smem, vmem, vmem],
+        out_specs=vmem,
+        compiler_params=pltpu.CompilerParams(vmem_limit_bytes=40 * 1024 * 1024),
+    )(counts, rows, cells.reshape(1, -1))
+
+
+GROUP = 8
+SLOTS = 1024
+
+
+def bin_kernel(got_ref, out_ref, rows_all, row_hot, col_hot, lhs, total):
+    sources, wide_rows, _ = got_ref.shape
+    columns = wide_rows - 16
+    _, tile_rows, tile_cols = out_ref.shape
+    step = pl.program_id(0)
+
+    @pl.when(step == 0)
+    def _():
+        row_id = lax.broadcasted_iota(jnp.int32, (tile_rows, CAP), 0)
+        col_id = lax.broadcasted_iota(jnp.int32, (tile_cols, CAP), 0)
+
+        def body(d, carry):
+            at = pl.ds(pl.multiple_of(d * CAP, CAP), CAP)
+            rows_all[:, at] = got_ref[d, 0:columns, :].astype(jnp.float32)
+            cells = got_ref[d, columns : columns + 16, :].astype(jnp.float32).astype(jnp.int32)
+            hot = jnp.where(row_id == cells[0:1, :], 1.0, 0.0)
+            row_hot[:, at] = hot.astype(jnp.bfloat16)
+            hot = jnp.where(col_id == cells[1:2, :], 1.0, 0.0)
+            col_hot[at, :] = hot.T.astype(jnp.bfloat16)
+            return carry
+
+        lax.fori_loop(0, sources, body, 0)
+
+    total[...] = jnp.zeros_like(total)
+    group_at = pl.ds(pl.multiple_of(step * GROUP, GROUP), GROUP)
+
+    def chunk(c, carry):
+        at = pl.ds(pl.multiple_of(c * SLOTS, SLOTS), SLOTS)
+        values = rows_all[group_at, at]
+        mask = row_hot[:, at]
+        for i in range(GROUP):
+            row = jnp.broadcast_to(values[i : i + 1, :], (tile_rows, SLOTS)).astype(jnp.bfloat16)
+            lhs[i * tile_rows : (i + 1) * tile_rows, :] = row * mask
+        total[...] += jnp.dot(lhs[...], col_hot[at, :], preferred_element_type=jnp.float32)
+        return carry
+
+    lax.fori_loop(0, (sources * CAP) // SLOTS, chunk, 0)
+    out_ref[...] = total[...].reshape(GROUP, tile_rows, tile_cols).astype(jnp.bfloat16)
+
+
+def bin_rows(got, columns, tile_rows, tile_cols):
+    slots = got.shape[0] * CAP
+    return pl.pallas_call(
+        bin_kernel,
+        grid=(columns // GROUP,),
+        out_shape=jax.ShapeDtypeStruct((columns, tile_rows, tile_cols), jnp.bfloat16),
+        in_specs=[pl.BlockSpec(got.shape, lambda i: (0, 0, 0))],
+        out_specs=pl.BlockSpec((GROUP, tile_rows, tile_cols), lambda i: (i, 0, 0)),
+        scratch_shapes=[
+            pltpu.VMEM((columns, slots), jnp.float32),
+            pltpu.VMEM((tile_rows, slots), jnp.bfloat16),
+            pltpu.VMEM((slots, tile_cols), jnp.bfloat16),
+            pltpu.VMEM((GROUP * tile_rows, SLOTS), jnp.bfloat16),
+            pltpu.VMEM((GROUP * tile_rows, tile_cols), jnp.float32),
+        ],
+        compiler_params=pltpu.CompilerParams(vmem_limit_bytes=40 * 1024 * 1024),
+    )(got)
+
+
 def per_device(omega, coefficients, obs_rows, obs_cell, obs_count):
     columns, tile_rows, tile_cols = omega.shape
     wide_count = lax.axis_size("wide")
@@ -66,32 +173,14 @@
         (((1,), (1,)), ((), ())),
         preferred_element_type=jnp.float32,
     )
-    summed = lax.psum(local_gram, ("wide", "gy"))
+    copies = jnp.broadcast_to(local_gram[None], (devices_all,) + local_gram.shape)
+    terms = lax.all_to_all(copies, ("wide", "gy"), split_axis=0, concat_axis=0, tiled=True)
+    summed = jnp.sum(terms, axis=0)
     gram = summed / (tile_rows * tile_cols * devices_all)
     counts_row = obs_count[0]
-    ends = jnp.cumsum(counts_row)
-    starts = ends - counts_row
-    padded_rows = jnp.pad(obs_rows, ((0, 0), (0, CAP)))
-    padded_cells = jnp.pad(obs_cell, (0, CAP))
-    slot_index = jnp.arange(CAP, dtype=jnp.int32)
-    positions = starts[:, None] + slot_index[None, :]
-    rows_win = jnp.transpose(jnp.take(padded_rows, positions, axis=1), (1, 0, 2))
-    cells_win = padded_cells[positions][:, None, :]
-    valid = (slot_index[None, :] < counts_row[:, None])[:, None, :]
-    send_rows = jnp.where(valid, rows_win, jnp.zeros((), jnp.bfloat16))
-    send_cells = jnp.where(valid, cells_win, tile_rows * tile_cols)
-    got_rows, got_cells = (
-        lax.all_to_all(send_rows, ("wide", "gy"), split_axis=0, concat_axis=0, tiled=True),
-        lax.all_to_all(send_cells, ("wide", "gy"), split_axis=0, concat_axis=0, tiled=True),
-    )
-    flat_rows = jnp.transpose(got_rows, (1, 0, 2)).reshape(columns, devices_all * CAP)
-    flat_cells = got_cells.reshape(devices_all * CAP)
-    binned = (
-        jnp.zeros((columns, tile_rows * tile_cols), jnp.float32)
-        .at[:, flat_cells]
-        .add(flat_rows.astype(jnp.float32), mode="drop")
-    )
-    data_field = binned.astype(jnp.bfloat16).reshape(columns, tile_rows, tile_cols)
+    packed = pack_windows(counts_row, obs_rows, obs_cell)
+    got = lax.all_to_all(packed, ("wide", "gy"), split_axis=0, concat_axis=0, tiled=True)
+    data_field = bin_rows(got, columns, tile_rows, tile_cols)
     return (applied, gram, data_field)
 
 

time: 309 us -> 240 us (0.78)
  local copies, waits for them, and re-layouts: 117 us -> 72.9 us
  blocking collectives: 40.7 us -> 0 us
  other arithmetic: 96.1 us -> 66.6 us
  waiting for transfers between devices: 1.74 us -> 27.1 us
  Pallas kernels: 0 us -> 23.2 us
  starting transfers between devices: 47 us -> 43.3 us
    psum x1 -> x0, blocking collectives: 40.7 us -> none  [per_device(): summed = lax.psum(local_gram, ('wide', 'gy'))]
    gather x3 -> x0, local copies, waits for them, and re-layouts: 35.6 us -> none  [the longest x1 23 us: per_device(): cells_win = padded_cells[positions][:, None, :]]
    scatter-add x1 -> x0, other arithmetic: 26.1 us -> none  [per_device(): binned = jnp.zeros((columns, tile_rows * tile_cols), jnp.float32).at[:, f...]
    pallas_call x0 -> x2, Pallas kernels: none -> 23.2 us  [the longest x1 18.8 us: bin_rows(): pl.pallas_call(bin_kernel, grid=(columns // GROUP,), out_shape=jax.ShapeD...]
    all_to_all x2, waiting for transfers between devices: 0.01 us -> 19.3 us  [the longest x1 11.1 us: per_device(): lax.all_to_all(copies, ('wide', 'gy'), split_axis=0, concat_axis=0, tiled...]
    ppermute x6, waiting for transfers between devices: 1.72 us -> 7.79 us  [with_halo(): lax.ppermute(lax.slice_in_dim(block, 0, width, axis=dim), axis, backward)]
    unnamed x25 -> x24, local copies, waits for them, and re-layouts: 20.5 us -> 15.3 us
    convert_element_type x2 -> x0, other arithmetic: 5.2 us -> none  [the longest x1 5.13 us: per_device(): binned.astype(jnp.bfloat16).reshape(columns, tile_rows, tile_cols)]
  transfers between devices with their start and end apart: 14 -> 14, of which waited for: 1 -> 5; matrix products, arithmetic and copies ran while one was open for 58% -> 17% of each run, Pallas kernels for 0% -> 2%
where the time goes in v1:
time: 240 us; the launch traced here: 238 us
  local copies, waits for them, and re-layouts  72.9 us (30%)
  other arithmetic  66.6 us (28%)
  starting transfers between devices  43.3 us (18%)
  waiting for transfers between devices  27.1 us (11%)
  Pallas kernels  23.2 us (10%)
  matrix products  4.06 us (2%)
    convert_element_type x1, other arithmetic, per_device(): applied = (0.0625 * second).astype(jnp.bfloat16)  25 us
    ppermute x6, starting transfers between devices, with_halo(): lax.ppermute(lax.slice_in_dim(block, block.shape[dim] - width, None, axis...  23.9 us
    convert_element_type x1, other arithmetic, per_device(): operator_apply(sketch_pad.astype(jnp.float32), coef_pad)  22.6 us
    pallas_call x1, Pallas kernels, bin_rows(): pl.pallas_call(bin_kernel, grid=(columns // GROUP,), out_shape=jax.ShapeD...  18.8 us
    unnamed x24, local copies, waits for them, and re-layouts  15.3 us
    slice x5, local copies, waits for them, and re-layouts, with_halo(): lax.slice_in_dim(block, block.shape[dim] - width, None, axis=dim)  15 us
    ppermute x2, local copies, waits for them, and re-layouts, with_halo(): lax.ppermute(lax.slice_in_dim(block, 0, width, axis=dim), axis, backward)  13.7 us
    ppermute x2, local copies, waits for them, and re-layouts, with_halo(): lax.ppermute(lax.slice_in_dim(block, block.shape[dim] - width, None, axis...  13.7 us
  transfers between devices with their start and end apart: 14, of which 5 were waited for; matrix products, arithmetic and copies ran while one was open for 17% of the time, Pallas kernels for 2%

profile of v1, /device:TPU:0, one launch (start us, length us, event | category | flops | bytes accessed | tf_op | source)
XLA Modules:
  0.0 238.3 jit_solution(8083929204172033222)
XLA Ops:
  0.6 0.8 fusion.29
  1.4 4.8 %collective-permute-start = (f32[4,1,256]{2,1,0:T(1,128)S(1)}, f32[4,1,256]{2,1,0:T(1,128)S(1)}, u32[]{:S(2)}, u32[]{:S(2)}) collective-permute-start(f32[4,1,256]{2,1,0:T(1,128)S(1)} %get-tuple-element.26), channel_id=1, source_target_pairs={{0,4},{4,8},{8,12},{12,16},{16,20},{20,24},{24,28},{1,5},{5,9},{9,... | collective-permute-start | bytes 12296 | tf_op jit(solution)/shard_map/ppermute | solution.py:16
  6.3 1.3 collective-permute-start.1
  7.6 0.0 collective-permute-done
  7.6 4.2 %collective-permute-done.1 = f32[4,1,256]{2,1,0:T(1,128)S(1)} collective-permute-done((f32[4,1,256]{2,1,0:T(1,128)S(1)}, f32[4,1,256]{2,1,0:T(1,128)S(1)}, u32[]{:S(2)}, u32[]{:S(2)}) %collective-permute-start.1) | collective-permute-done | bytes 4128 | tf_op jit(solution)/shard_map/ppermute | solution.py:19
  11.8 1.0 pad_maximum_fusion.1
  12.7 0.1 fusion.28
  12.8 1.3 collective-permute-start.2
  14.1 1.3 collective-permute-start.3
  15.4 1.1 fusion.27
  16.6 4.4 %collective-permute-start.4 = (bf16[64,1,256]{2,0,1:T(8,128)(2,1)S(1)}, bf16[64,1,256]{2,0,1:T(8,128)(2,1)S(1)}, u32[]{:S(2)}, u32[]{:S(2)}) collective-permute-start(bf16[64,1,256]{2,0,1:T(8,128)(2,1)S(1)} %copy.74), channel_id=1, source_target_pairs={{0,4},{4,8},{8,12},{12,16},{16,20},{20,24},{24,28},{1,5},{5,9},{9,... | collective-permute-start | bytes 98312 | tf_op jit(solution)/shard_map/ppermute | solution.py:16
  21.0 1.3 collective-permute-start.5
  22.3 7.5 %copy.53 = bf16[64,64,256]{1,0,2:T(8,128)(2,1)} copy(bf16[64,64,256]{2,1,0:T(8,128)(2,1)} %param.5) | data formatting | bytes 4194304 | tf_op args[0]
  29.8 1.2 pad_maximum_fusion
  31.1 0.2 fusion.22
  31.2 6.8 %copy.52 = bf16[64,1,256]{1,0,2:T(8,128)(2,1)} copy(bf16[64,1,256]{2,0,1:T(8,128)(2,1)S(1)} %collective-permute-done.4) | data formatting | bytes 65536 | tf_op jit(solution)/shard_map/ppermute | solution.py:16
  38.1 6.8 %copy.54 = bf16[64,1,256]{1,0,2:T(8,128)(2,1)} copy(bf16[64,1,256]{2,0,1:T(8,128)(2,1)S(1)} %collective-permute-done.5) | data formatting | bytes 65536 | tf_op jit(solution)/shard_map/ppermute | solution.py:19
  44.9 0.9 pad_maximum_fusion.7
  45.8 4.5 %collective-permute-start.6 = (bf16[64,66,1]{1,0,2:T(8,128)(2,1)S(1)}, bf16[64,66,1]{1,0,2:T(8,128)(2,1)S(1)}, u32[]{:S(2)}, u32[]{:S(2)}) collective-permute-start(bf16[64,66,1]{1,0,2:T(8,128)(2,1)S(1)} %get-tuple-element.14), channel_id=1, source_target_pairs={{0,1},{1,2},{2,3},{4,5},{5,6},{6,7},{8,9},{9,10},{10,11},{12,13},{... | collective-permute-start | bytes 25352 | tf_op jit(solution)/shard_map/ppermute | solution.py:16
  50.3 1.5 collective-permute-start.7
  51.8 0.1 fusion.30
  51.9 0.1 copy.55
  52.0 0.1 copy.56
  52.1 0.1 copy.57
  52.2 0.1 copy.58
  52.3 0.1 copy.59
  52.4 0.1 copy.60
  52.5 0.1 copy.61
  52.6 0.1 copy.62
  52.7 0.1 slice.210
  52.8 0.1 copy.49
  52.9 2.0 collective-permute-done.7
  54.9 6.6 %maximum_convert_fusion = f32[64,66,258]{1,0,2:T(8,128)S(1)} fusion(bf16[64,66,1]{1,0,2:T(8,128)(2,1)S(1)} %collective-permute-done.7, bf16[64,1,256]{1,0,2:T(8,128)(2,1)} %copy.54, bf16[64,64,256]{1,0,2:T(8,128)(2,1)} %copy.53, bf16[64,1,256]{1,0,2:T(8,128)(2,1)} %copy.52, bf16[64,66,1]{1,0,2:T(8,128)(2,1)S(1)} %collective-permute-done.6), kind=kLoop, calls=%fused_computation.29 | loop fusion | flops 10897920 | bytes 6538752 | tf_op jit(solution)/shard_map/convert_element_type | solution.py:165
  61.5 22.6 %fusion.15 = bf16[64,64,256]{1,0,2:T(8,128)(2,1)} fusion(f32[64,66,258]{1,0,2:T(8,128)S(1)} %maximum_convert_fusion, f32[64,256]{0,1:T(8,128)S(1)} %copy.62, f32[64,256]{0,1:T(8,128)S(1)} %copy.61, f32[64,256]{0,1:T(8,128)S(1)} %copy.60, f32[64,256]{0,1:T(8,128)S(1)} %copy.59, f32[64,256]{0,1:T(8,128)S(1)} %copy.58, f32[64,256]{0,1:T(8,128)S(1)} %copy.57, ...), kind=kLoop, calls=%fused_computation.20 | loop fusion | flops 28311552 | bytes 40435712 | tf_op jit(solution)/shard_map/convert_element_type | solution.py:165
  84.1 7.4 %fusion.26 = (bf16[64,1,256]{1,0,2:T(8,128)(2,1)}, bf16[64,1,256]{1,0,2:T(8,128)(2,1)}) fusion(bf16[64,64,256]{1,0,2:T(8,128)(2,1)} %fusion.15), kind=kLoop, calls=%fused_computation.54 | loop fusion | bytes 131072 | tf_op jit(solution)/shard_map/slice | solution.py:17
  91.5 5.6 %copy.63 = bf16[64,1,256]{2,0,1:T(8,128)(2,1)S(1)} copy(bf16[64,1,256]{1,0,2:T(8,128)(2,1)} %get-tuple-element.16) | data formatting | bytes 65536 | tf_op jit(solution)/shard_map/slice | solution.py:17
  97.1 4.5 %collective-permute-start.8 = (bf16[64,1,256]{2,0,1:T(8,128)(2,1)S(1)}, bf16[64,1,256]{2,0,1:T(8,128)(2,1)S(1)}, u32[]{:S(2)}, u32[]{:S(2)}) collective-permute-start(bf16[64,1,256]{2,0,1:T(8,128)(2,1)S(1)} %copy.63), channel_id=1, source_target_pairs={{0,4},{4,8},{8,12},{12,16},{16,20},{20,24},{24,28},{1,5},{5,9},{9,... | collective-permute-start | bytes 98312 | tf_op jit(solution)/shard_map/ppermute | solution.py:16
  101.6 5.6 %copy.64 = bf16[64,1,256]{2,0,1:T(8,128)(2,1)S(1)} copy(bf16[64,1,256]{1,0,2:T(8,128)(2,1)} %get-tuple-element.17) | data formatting | bytes 65536 | tf_op jit(solution)/shard_map/slice | solution.py:19
  107.2 1.3 collective-permute-start.9
  108.5 6.8 %copy.65 = bf16[64,1,256]{1,0,2:T(8,128)(2,1)} copy(bf16[64,1,256]{2,0,1:T(8,128)(2,1)S(1)} %collective-permute-done.8) | data formatting | bytes 65536 | tf_op jit(solution)/shard_map/ppermute | solution.py:16
  115.4 6.9 %copy.66 = bf16[64,1,256]{1,0,2:T(8,128)(2,1)} copy(bf16[64,1,256]{2,0,1:T(8,128)(2,1)S(1)} %collective-permute-done.9) | data formatting | bytes 65536 | tf_op jit(solution)/shard_map/ppermute | solution.py:19
  122.3 1.0 pad_maximum_fusion.4
  123.3 4.4 %collective-permute-start.10 = (bf16[64,66,1]{1,0,2:T(8,128)(2,1)S(1)}, bf16[64,66,1]{1,0,2:T(8,128)(2,1)S(1)}, u32[]{:S(2)}, u32[]{:S(2)}) collective-permute-start(bf16[64,66,1]{1,0,2:T(8,128)(2,1)S(1)} %get-tuple-element.12), channel_id=1, source_target_pairs={{0,1},{1,2},{2,3},{4,5},{5,6},{6,7},{8,9},{9,10},{10,11},{12,13},{... | collective-permute-start | bytes 25352 | tf_op jit(solution)/shard_map/ppermute | solution.py:16
  127.7 1.5 collective-permute-start.11
  129.2 1.6 collective-permute-done.11
  130.9 5.6 %maximum_convert_fusion.1 = f32[64,66,258]{1,0,2:T(8,128)S(1)} fusion(bf16[64,66,1]{1,0,2:T(8,128)(2,1)S(1)} %collective-permute-done.11, bf16[64,1,256]{1,0,2:T(8,128)(2,1)S(1)} %copy-done.4, bf16[64,64,256]{1,0,2:T(8,128)(2,1)S(1)} %copy-done.2, bf16[64,1,256]{1,0,2:T(8,128)(2,1)S(1)} %copy-done.3, bf16[64,66,1]{1,0,2:T(8,128)(2,1)S(1)} %collective-permute-done.10), kind=kLoop, calls=%fused_computation.30 | loop fusion | flops 10897920 | bytes 6538752 | tf_op jit(solution)/shard_map/convert_element_type | solution.py:168
  136.5 25.0 %fusion.5 = bf16[64,64,256]{1,0,2:T(8,128)(2,1)} fusion(f32[64,66,258]{1,0,2:T(8,128)S(1)} %maximum_convert_fusion.1, f32[64,256]{0,1:T(8,128)} %copy-done.6, f32[64,256]{0,1:T(8,128)S(1)} %copy.61, f32[64,256]{0,1:T(8,128)S(1)} %copy.60, f32[64,256]{0,1:T(8,128)S(1)} %copy.59, f32[64,256]{0,1:T(8,128)S(1)} %copy.58, f32[64,256]{0,1:T(8,128)S(1)} %copy.57, ...), kind=kLoop, calls=%fused_computation.6 | loop fusion | flops 29360128 | bytes 40435712 | tf_op jit(solution)/shard_map/convert_element_type | solution.py:169
  161.5 7.8 %copy.67 = bf16[64,64,256]{2,0,1:T(8,128)(2,1)} copy(bf16[64,64,256]{1,0,2:T(8,128)(2,1)} %fusion.5) | data formatting | bytes 4194304 | tf_op jit(solution)/shard_map/convert_element_type | solution.py:169
  169.3 4.1 %convolution_bitcast_fusion = f32[64,64]{0,1:T(8,128)S(1)} fusion(bf16[64,64,256]{2,0,1:T(8,128)(2,1)} %copy.67, bf16[64,64,256]{2,1,0:T(8,128)(2,1)S(1)} %copy-done.5), kind=kOutput, calls=%fused_computation.31 | convolution fusion | flops 134217728 | bytes 4210688 | tf_op jit(solution)/shard_map/dot_general | solution.py:170
  173.4 0.1 copy.69
  173.5 0.1 broadcast_in_dim.2
  173.6 1.5 reshape.23
  175.1 7.9 %all-to-all-start = ((f32[32,1,4096]{2,1,0:T(1,128)}), f32[32,1,4096]{2,1,0:T(1,128)S(1)}, u32[]{:S(2)}, u32[]{:S(2)}) async-start(f32[32,1,4096]{2,1,0:T(1,128)} %reshape.23), calls=%async_computation | async-start | bytes 1048576 | tf_op jit(solution)/shard_map/all_to_all | solution.py:177
  183.0 4.4 %shard_map.76 = bf16[32,80,128]{2,1,0:T(8,128)(2,1)} custom-call(s32[32]{0:T(128)S(1)} %bitcast.14, bf16[64,3200]{1,0:T(8,128)(2,1)S(1)} %copy-done, s32[1,3200]{1,0:T(1,128)S(1)} %reshape.21.cells_ref), custom_call_target="tpu_custom_call" | custom-call | tf_op jit(solution)/shard_map/pallas_call | solution.py:86
  187.4 11.1 %all-to-all-done = f32[32,1,4096]{2,1,0:T(1,128)S(1)} async-done(((f32[32,1,4096]{2,1,0:T(1,128)}), f32[32,1,4096]{2,1,0:T(1,128)S(1)}, u32[]{:S(2)}, u32[]{:S(2)}) %all-to-all-start) | async-done | bytes 524320 | tf_op jit(solution)/shard_map/all_to_all | solution.py:177
  198.5 3.3 %all-to-all-start.1 = ((bf16[32,80,128]{2,1,0:T(8,128)(2,1)}), bf16[32,80,128]{2,1,0:T(8,128)(2,1)S(1)}, u32[]{:S(2)}, u32[]{:S(2)}) async-start(bf16[32,80,128]{2,1,0:T(8,128)(2,1)} %shard_map.76), calls=%async_computation.1 | async-start | bytes 1310720 | tf_op jit(solution)/shard_map/all_to_all | solution.py:182
  201.9 5.9 %copy.70 = bf16[64,64,256]{2,1,0:T(8,128)(2,1)} copy(bf16[64,64,256]{1,0,2:T(8,128)(2,1)} %fusion.5) | data formatting | bytes 4194304
  207.8 0.5 broadcast.25
  208.3 1.9 reduce
  210.2 0.4 reshape.24
  210.6 0.1 reduce_sum.9
  210.7 0.6 broadcast_multiply_fusion
  211.3 8.2 %all-to-all-done.1.got_ref = bf16[32,80,128]{2,1,0:T(8,128)(2,1)S(1)} async-done(((bf16[32,80,128]{2,1,0:T(8,128)(2,1)}), bf16[32,80,128]{2,1,0:T(8,128)(2,1)S(1)}, u32[]{:S(2)}, u32[]{:S(2)}) %all-to-all-start.1) | async-done | bytes 655392 | tf_op jit(solution)/shard_map/all_to_all | solution.py:182
  219.5 18.8 %shard_map.77 = bf16[64,64,256]{2,1,0:T(8,128)(2,1)} custom-call(bf16[32,80,128]{2,1,0:T(8,128)(2,1)S(1)} %all-to-all-done.1.got_ref), custom_call_target="tpu_custom_call" | custom-call | tf_op jit(solution)/shard_map/pallas_call | solution.py:141
  (30 shorter events, 0.1 us)
Async XLA Ops:
  1.4 6.1 %collective-permute-start = (f32[4,1,256]{2,1,0:T(1,128)S(1)}, f32[4,1,256]{2,1,0:T(1,128)S(1)}, u32[]{:S(2)}, u32[]{:S(2)}) collective-permute-start(f32[4,1,256]{2,1,0:T(1,128)S(1)} %get-tuple-element.26), channel_id=1, source_target_pairs={{0,4},{4,8},{8,12},{12,16},{16,20},{20,24},{24,28},{1,5},{5,9},{9,... | collective-permute-start | bytes 12296 | tf_op jit(solution)/shard_map/ppermute | solution.py:16
  6.3 5.5 %collective-permute-start.1 = (f32[4,1,256]{2,1,0:T(1,128)S(1)}, f32[4,1,256]{2,1,0:T(1,128)S(1)}, u32[]{:S(2)}, u32[]{:S(2)}) collective-permute-start(f32[4,1,256]{2,1,0:T(1,128)S(1)} %get-tuple-element.27), channel_id=1, source_target_pairs={{4,0},{8,4},{12,8},{16,12},{20,16},{24,20},{28,24},{5,1},{9,5},{13... | collective-permute-start | bytes 12296 | tf_op jit(solution)/shard_map/ppermute | solution.py:19
  12.8 17.0 %collective-permute-start.2 = (f32[4,66,1]{2,1,0:T(8,128)S(1)}, f32[4,66,1]{2,1,0:T(8,128)S(1)}, u32[]{:S(2)}, u32[]{:S(2)}) collective-permute-start(f32[4,66,1]{2,1,0:T(8,128)S(1)} %get-tuple-element.24), channel_id=1, source_target_pairs={{0,1},{1,2},{2,3},{4,5},{5,6},{6,7},{8,9},{9,10},{10,11},{12,13},{... | collective-permute-start | bytes 3176 | tf_op jit(solution)/shard_map/ppermute | solution.py:16
  14.1 15.7 %collective-permute-start.3 = (f32[4,66,1]{2,1,0:T(8,128)S(1)}, f32[4,66,1]{2,1,0:T(8,128)S(1)}, u32[]{:S(2)}, u32[]{:S(2)}) collective-permute-start(f32[4,66,1]{2,1,0:T(8,128)S(1)} %get-tuple-element.25), channel_id=1, source_target_pairs={{1,0},{2,1},{3,2},{5,4},{6,5},{7,6},{9,8},{10,9},{11,10},{13,12},{... | collective-permute-start | bytes 3176 | tf_op jit(solution)/shard_map/ppermute | solution.py:19
  16.6 14.6 %collective-permute-start.4 = (bf16[64,1,256]{2,0,1:T(8,128)(2,1)S(1)}, bf16[64,1,256]{2,0,1:T(8,128)(2,1)S(1)}, u32[]{:S(2)}, u32[]{:S(2)}) collective-permute-start(bf16[64,1,256]{2,0,1:T(8,128)(2,1)S(1)} %copy.74), channel_id=1, source_target_pairs={{0,4},{4,8},{8,12},{12,16},{16,20},{20,24},{24,28},{1,5},{5,9},{9,... | collective-permute-start | bytes 98312 | tf_op jit(solution)/shard_map/ppermute | solution.py:16
  21.0 17.1 %collective-permute-start.5 = (bf16[64,1,256]{2,0,1:T(8,128)(2,1)S(1)}, bf16[64,1,256]{2,0,1:T(8,128)(2,1)S(1)}, u32[]{:S(2)}, u32[]{:S(2)}) collective-permute-start(bf16[64,1,256]{2,0,1:T(8,128)(2,1)S(1)} %copy.73), channel_id=1, source_target_pairs={{4,0},{8,4},{12,8},{16,12},{20,16},{24,20},{28,24},{5,1},{9,5},{13... | collective-permute-start | bytes 98312 | tf_op jit(solution)/shard_map/ppermute | solution.py:19
  45.8 7.1 %collective-permute-start.6 = (bf16[64,66,1]{1,0,2:T(8,128)(2,1)S(1)}, bf16[64,66,1]{1,0,2:T(8,128)(2,1)S(1)}, u32[]{:S(2)}, u32[]{:S(2)}) collective-permute-start(bf16[64,66,1]{1,0,2:T(8,128)(2,1)S(1)} %get-tuple-element.14), channel_id=1, source_target_pairs={{0,1},{1,2},{2,3},{4,5},{5,6},{6,7},{8,9},{9,10},{10,11},{12,13},{... | collective-permute-start | bytes 25352 | tf_op jit(solution)/shard_map/ppermute | solution.py:16
  50.3 4.6 %collective-permute-start.7 = (bf16[64,66,1]{1,0,2:T(8,128)(2,1)S(1)}, bf16[64,66,1]{1,0,2:T(8,128)(2,1)S(1)}, u32[]{:S(2)}, u32[]{:S(2)}) collective-permute-start(bf16[64,66,1]{1,0,2:T(8,128)(2,1)S(1)} %get-tuple-element.15), channel_id=1, source_target_pairs={{1,0},{2,1},{3,2},{5,4},{6,5},{7,6},{9,8},{10,9},{11,10},{13,12},{... | collective-permute-start | bytes 25352 | tf_op jit(solution)/shard_map/ppermute | solution.py:19
  52.7 8.8 %copy-start.6 = (f32[64,256]{0,1:T(8,128)}, f32[64,256]{0,1:T(8,128)S(1)}, u32[]{:S(2)}) copy-start(f32[64,256]{0,1:T(8,128)S(1)} %copy.62) | copy-start | bytes 196612
  52.9 8.6 %copy-start.7 = (f32[64,256]{0,1:T(8,128)}, f32[64,256]{0,1:T(8,128)S(1)}, u32[]{:S(2)}) copy-start(f32[64,256]{0,1:T(8,128)S(1)} %copy.49) | copy-start | bytes 196612
  97.1 11.5 %collective-permute-start.8 = (bf16[64,1,256]{2,0,1:T(8,128)(2,1)S(1)}, bf16[64,1,256]{2,0,1:T(8,128)(2,1)S(1)}, u32[]{:S(2)}, u32[]{:S(2)}) collective-permute-start(bf16[64,1,256]{2,0,1:T(8,128)(2,1)S(1)} %copy.63), channel_id=1, source_target_pairs={{0,4},{4,8},{8,12},{12,16},{16,20},{20,24},{24,28},{1,5},{5,9},{9,... | collective-permute-start | bytes 98312 | tf_op jit(solution)/shard_map/ppermute | solution.py:16
  107.2 8.2 %collective-permute-start.9 = (bf16[64,1,256]{2,0,1:T(8,128)(2,1)S(1)}, bf16[64,1,256]{2,0,1:T(8,128)(2,1)S(1)}, u32[]{:S(2)}, u32[]{:S(2)}) collective-permute-start(bf16[64,1,256]{2,0,1:T(8,128)(2,1)S(1)} %copy.64), channel_id=1, source_target_pairs={{4,0},{8,4},{12,8},{16,12},{20,16},{24,20},{28,24},{5,1},{9,5},{13... | collective-permute-start | bytes 98312 | tf_op jit(solution)/shard_map/ppermute | solution.py:19
  122.3 8.6 %copy-start.2 = (bf16[64,64,256]{1,0,2:T(8,128)(2,1)S(1)}, bf16[64,64,256]{1,0,2:T(8,128)(2,1)}, u32[]{:S(2)}) copy-start(bf16[64,64,256]{1,0,2:T(8,128)(2,1)} %fusion.15) | copy-start | bytes 6291460
  122.3 8.6 %copy-start.3 = (bf16[64,1,256]{1,0,2:T(8,128)(2,1)S(1)}, bf16[64,1,256]{1,0,2:T(8,128)(2,1)}, u32[]{:S(2)}) copy-start(bf16[64,1,256]{1,0,2:T(8,128)(2,1)} %copy.65) | copy-start | bytes 98308
  122.3 8.6 %copy-start.4 = (bf16[64,1,256]{1,0,2:T(8,128)(2,1)S(1)}, bf16[64,1,256]{1,0,2:T(8,128)(2,1)}, u32[]{:S(2)}) copy-start(bf16[64,1,256]{1,0,2:T(8,128)(2,1)} %copy.66) | copy-start | bytes 98308
  123.3 5.9 %collective-permute-start.10 = (bf16[64,66,1]{1,0,2:T(8,128)(2,1)S(1)}, bf16[64,66,1]{1,0,2:T(8,128)(2,1)S(1)}, u32[]{:S(2)}, u32[]{:S(2)}) collective-permute-start(bf16[64,66,1]{1,0,2:T(8,128)(2,1)S(1)} %get-tuple-element.12), channel_id=1, source_target_pairs={{0,1},{1,2},{2,3},{4,5},{5,6},{6,7},{8,9},{9,10},{10,11},{12,13},{... | collective-permute-start | bytes 25352 | tf_op jit(solution)/shard_map/ppermute | solution.py:16
  127.7 3.2 %collective-permute-start.11 = (bf16[64,66,1]{1,0,2:T(8,128)(2,1)S(1)}, bf16[64,66,1]{1,0,2:T(8,128)(2,1)S(1)}, u32[]{:S(2)}, u32[]{:S(2)}) collective-permute-start(bf16[64,66,1]{1,0,2:T(8,128)(2,1)S(1)} %get-tuple-element.13), channel_id=1, source_target_pairs={{1,0},{2,1},{3,2},{5,4},{6,5},{7,6},{9,8},{10,9},{11,10},{13,12},{... | collective-permute-start | bytes 25352 | tf_op jit(solution)/shard_map/ppermute | solution.py:19
  136.4 32.9 %copy-start.5 = (bf16[64,64,256]{2,1,0:T(8,128)(2,1)S(1)}, bf16[64,64,256]{2,1,0:T(8,128)(2,1)}, u32[]{:S(2)}) copy-start(bf16[64,64,256]{2,1,0:T(8,128)(2,1)} %param.5) | copy-start | bytes 6291460
  161.5 21.5 %copy-start.8 = (s32[3200]{0:T(1024)S(1)}, s32[3200]{0:T(1024)}, u32[]{:S(2)}) copy-start(s32[3200]{0:T(1024)} %param.8) | copy-start | bytes 38404
  161.5 21.5 %copy-start = (bf16[64,3200]{1,0:T(8,128)(2,1)S(1)}, bf16[64,3200]{1,0:T(8,128)(2,1)}, u32[]{:S(2)}) copy-start(bf16[64,3200]{1,0:T(8,128)(2,1)} %rows_ref.1) | copy-start | bytes 1228804
  161.5 21.5 %copy-start.1 = (s32[1,32]{1,0:T(1,128)S(1)}, s32[1,32]{1,0:T(1,128)}, u32[]{:S(2)}) copy-start(s32[1,32]{1,0:T(1,128)} %param.9) | copy-start | bytes 388
  175.1 23.5 %all-to-all-start = ((f32[32,1,4096]{2,1,0:T(1,128)}), f32[32,1,4096]{2,1,0:T(1,128)S(1)}, u32[]{:S(2)}, u32[]{:S(2)}) async-start(f32[32,1,4096]{2,1,0:T(1,128)} %reshape.23), calls=%async_computation | async-start | bytes 1048576 | tf_op jit(solution)/shard_map/all_to_all | solution.py:177
  198.5 21.0 %all-to-all-start.1 = ((bf16[32,80,128]{2,1,0:T(8,128)(2,1)}), bf16[32,80,128]{2,1,0:T(8,128)(2,1)S(1)}, u32[]{:S(2)}, u32[]{:S(2)}) async-start(bf16[32,80,128]{2,1,0:T(8,128)(2,1)} %shard_map.76), calls=%async_computation.1 | async-start | bytes 1310720 | tf_op jit(solution)/shard_map/all_to_all | solution.py:182

commit v2 on v1

--- a/solution.py
+++ b/solution.py
@@ -1,3 +1,5 @@
+import functools
+
 import jax
 import jax.numpy as jnp
 from jax import lax
@@ -21,33 +23,83 @@
     return block
 
 
-def operator_apply(field, coef):
-    kappa_sq = coef[0]
-    cond_rows = coef[1]
-    cond_cols = coef[2]
-    cond_cross = coef[3]
-    centre = field[..., 1:-1, 1:-1]
-    face_south = 0.5 * (cond_rows[1:-1, 1:-1] + cond_rows[2:, 1:-1])
-    face_north = 0.5 * (cond_rows[1:-1, 1:-1] + cond_rows[:-2, 1:-1])
-    face_east = 0.5 * (cond_cols[1:-1, 1:-1] + cond_cols[1:-1, 2:])
-    face_west = 0.5 * (cond_cols[1:-1, 1:-1] + cond_cols[1:-1, :-2])
-    diffusion = face_south * (field[..., 2:, 1:-1] - centre) - face_north * (
-        centre - field[..., :-2, 1:-1]
-    )
-    diffusion = (
-        diffusion
-        + face_east * (field[..., 1:-1, 2:] - centre)
-        - face_west * (centre - field[..., 1:-1, :-2])
-    )
-    mixed = cond_cross[2:, 1:-1] * (field[..., 2:, 2:] - field[..., 2:, :-2]) - cond_cross[
-        :-2, 1:-1
-    ] * (field[..., :-2, 2:] - field[..., :-2, :-2])
-    mixed = (
-        mixed
-        + cond_cross[1:-1, 2:] * (field[..., 2:, 2:] - field[..., :-2, 2:])
-        - cond_cross[1:-1, :-2] * (field[..., 2:, :-2] - field[..., :-2, :-2])
-    )
-    return kappa_sq[1:-1, 1:-1] * centre - diffusion - 0.25 * mixed
+def halo_of(block, sides):
+    parts = []
+    for axis, dim in sides:
+        count = lax.axis_size(axis)
+        forward = [(i, i + 1) for i in range(count - 1)]
+        backward = [(target, source) for source, target in forward]
+        first = lax.slice_in_dim(block, 0, 1, axis=dim)
+        last = lax.slice_in_dim(block, block.shape[dim] - 1, None, axis=dim)
+        if parts:
+            north, south = parts
+            cut = lambda a, at: lax.slice_in_dim(a, at, at + 1, axis=dim)
+            end = block.shape[dim] - 1
+            first = jnp.concatenate([cut(north, 0), first, cut(south, 0)], axis=dim - 1)
+            last = jnp.concatenate([cut(north, end), last, cut(south, end)], axis=dim - 1)
+        low = lax.ppermute(last, axis, forward)
+        high = lax.ppermute(first, axis, backward)
+        parts = parts + [low, high]
+    return parts
+
+
+def stencil_planes(coef):
+    def face(c, di, dj):
+        near = c[1 + di : c.shape[0] - 1 + di, 1 + dj : c.shape[1] - 1 + dj]
+        return near
+
+    rows, cols, cross = coef[1], coef[2], coef[3]
+    south = 0.5 * (face(rows, 0, 0) + face(rows, 1, 0))
+    north = 0.5 * (face(rows, 0, 0) + face(rows, -1, 0))
+    east = 0.5 * (face(cols, 0, 0) + face(cols, 0, 1))
+    west = 0.5 * (face(cols, 0, 0) + face(cols, 0, -1))
+    cs, cn = 0.25 * face(cross, 1, 0), 0.25 * face(cross, -1, 0)
+    ce, cw = 0.25 * face(cross, 0, 1), 0.25 * face(cross, 0, -1)
+    centre = face(coef[0], 0, 0) + south + north + east + west
+    return jnp.stack(
+        [-(cn + cw), -north, cn + ce, -west, centre, -east, cs + cw, -south, -(cs + ce)]
+    )
+
+
+def stencil_kernel(scale, planes, field, north, south, west, east, out):
+    group, tile_rows, tile_cols = field.shape
+    row = lax.broadcasted_iota(jnp.int32, (tile_rows, tile_cols), 0)
+    col = lax.broadcasted_iota(jnp.int32, (tile_rows, tile_cols), 1)
+    for k in range(group):
+        v = field[k].astype(jnp.float32)
+        top = north[k].astype(jnp.float32)
+        bottom = south[k].astype(jnp.float32)
+        low = west[k].astype(jnp.float32)
+        high = east[k].astype(jnp.float32)
+        up = jnp.where(row == 0, top, pltpu.roll(v, 1, 0))
+        down = jnp.where(row == tile_rows - 1, bottom, pltpu.roll(v, tile_rows - 1, 0))
+        total = None
+        for i, line in enumerate((up, v, down)):
+            left = jnp.where(col == 0, low[i : i + tile_rows], pltpu.roll(line, 1, 1))
+            right = jnp.where(
+                col == tile_cols - 1,
+                high[i : i + tile_rows],
+                pltpu.roll(line, tile_cols - 1, 1),
+            )
+            term = planes[3 * i] * left + planes[3 * i + 1] * line + planes[3 * i + 2] * right
+            total = term if total is None else total + term
+        out[k] = (scale * total).astype(jnp.bfloat16)
+
+
+def stencil(field, planes, scale):
+    columns, tile_rows, tile_cols = field.shape
+    sides = halo_of(field, (("wide", 1), ("gy", 2)))
+    group = 8
+    by_column = lambda a: pl.BlockSpec((group,) + a.shape[1:], lambda i: (i, 0, 0))
+    return pl.pallas_call(
+        functools.partial(stencil_kernel, scale),
+        grid=(columns // group,),
+        out_shape=jax.ShapeDtypeStruct(field.shape, jnp.bfloat16),
+        in_specs=[pl.BlockSpec(planes.shape, lambda i: (0, 0, 0)), by_column(field)]
+        + [by_column(a) for a in sides],
+        out_specs=by_column(field),
+        compiler_params=pltpu.CompilerParams(vmem_limit_bytes=40 * 1024 * 1024),
+    )(planes, field, *sides)
 
 
 def pack_kernel(counts_ref, rows_ref, cells_ref, out_ref):
@@ -161,12 +213,9 @@
     gy_count = lax.axis_size("gy")
     devices_all = wide_count * gy_count
     coef_pad = with_halo(coefficients, (("wide", 1), ("gy", 2)), 1)
-    sketch_pad = with_halo(omega, (("wide", 1), ("gy", 2)), 1)
-    image = operator_apply(sketch_pad.astype(jnp.float32), coef_pad).astype(jnp.bfloat16)
-    image = lax.optimization_barrier(image)
-    image_pad = with_halo(image, (("wide", 1), ("gy", 2)), 1)
-    second = operator_apply(image_pad.astype(jnp.float32), coef_pad)
-    applied = (0.0625 * second).astype(jnp.bfloat16)
+    planes = stencil_planes(coef_pad)
+    image = stencil(omega, planes, 1.0)
+    applied = stencil(image, planes, 0.0625)
     local_gram = lax.dot_general(
         omega.reshape(columns, tile_rows * tile_cols),
         applied.reshape(columns, tile_rows * tile_cols),

time: 240 us -> 157 us (0.65)
  other arithmetic: 66.6 us -> 5.12 us
  local copies, waits for them, and re-layouts: 72.9 us -> 26.4 us
  Pallas kernels: 23.2 us -> 41.1 us
  waiting for transfers between devices: 27.1 us -> 32 us
    convert_element_type x4 -> x0, other arithmetic: 59.8 us -> none  [the longest x1 25 us: per_device(): applied = (0.0625 * second).astype(jnp.bfloat16)]
    ppermute x0 -> x8, starting transfers between devices: none -> 24 us  [the longest x4 18.9 us: halo_of(): low = lax.ppermute(last, axis, forward)]
    ppermute x4, local copies, waits for them, and re-layouts: 27.4 us -> 4.37 us  [the longest x2 2.18 us: halo_of(): high = lax.ppermute(first, axis, backward)]
    pallas_call x0 -> x2, Pallas kernels: none -> 17.9 us  [stencil(): pl.pallas_call(functools.partial(stencil_kernel, scale), grid=(columns //...]
    ppermute x6 -> x2, starting transfers between devices: 23.9 us -> 6.13 us  [with_halo(): lax.ppermute(lax.slice_in_dim(block, block.shape[dim] - width, None, axis...]
    slice x5 -> x2, local copies, waits for them, and re-layouts: 15 us -> 0.88 us  [with_halo(): lax.slice_in_dim(block, block.shape[dim] - width, None, axis=dim)]
    convert_element_type x1 -> x0, local copies, waits for them, and re-layouts: 7.83 us -> none  [per_device(): applied = (0.0625 * second).astype(jnp.bfloat16)]
    ppermute x6 -> x2, waiting for transfers between devices: 7.79 us -> 0.75 us  [with_halo(): lax.ppermute(lax.slice_in_dim(block, 0, width, axis=dim), axis, backward)]
  transfers between devices with their start and end apart: 14 -> 14, of which waited for: 5 -> 5; matrix products, arithmetic and copies ran while one was open for 17% -> 12% of each run, Pallas kernels for 2% -> 3%
where the time goes in v2:
time: 157 us; the launch traced here: 156 us
  starting transfers between devices  44.2 us (28%)
  Pallas kernels  41.1 us (26%)
  waiting for transfers between devices  32 us (20%)
  local copies, waits for them, and re-layouts  26.4 us (17%)
  matrix products  6.01 us (4%)
  other arithmetic  5.12 us (3%)
    ppermute x4, starting transfers between devices, halo_of(): low = lax.ppermute(last, axis, forward)  18.9 us
    pallas_call x1, Pallas kernels, bin_rows(): pl.pallas_call(bin_kernel, grid=(columns // GROUP,), out_shape=jax.ShapeD...  18.8 us
    pallas_call x2, Pallas kernels, stencil(): pl.pallas_call(functools.partial(stencil_kernel, scale), grid=(columns //...  17.9 us
    all_to_all x1, waiting for transfers between devices, per_device(): lax.all_to_all(packed, ('wide', 'gy'), split_axis=0, concat_axis=0, tiled...  14.4 us
    all_to_all x1, waiting for transfers between devices, per_device(): lax.all_to_all(copies, ('wide', 'gy'), split_axis=0, concat_axis=0, tiled...  11.1 us
    unnamed x26, local copies, waits for them, and re-layouts  9.1 us
    all_to_all x1, starting transfers between devices, per_device(): lax.all_to_all(copies, ('wide', 'gy'), split_axis=0, concat_axis=0, tiled...  8.4 us
    slice x5, local copies, waits for them, and re-layouts, halo_of(): first = lax.slice_in_dim(block, 0, 1, axis=dim)  6.46 us
  transfers between devices with their start and end apart: 14, of which 5 were waited for; matrix products, arithmetic and copies ran while one was open for 12% of the time, Pallas kernels for 3%

profile of v2, /device:TPU:0, one launch (start us, length us, event | category | flops | bytes accessed | tf_op | source)
XLA Modules:
  0.0 155.9 jit_solution(12981630648106755753)
XLA Ops:
  0.6 0.8 fusion.22
  1.4 4.8 %collective-permute-start = (f32[4,1,256]{2,1,0:T(1,128)S(1)}, f32[4,1,256]{2,1,0:T(1,128)S(1)}, u32[]{:S(2)}, u32[]{:S(2)}) collective-permute-start(f32[4,1,256]{2,1,0:T(1,128)S(1)} %get-tuple-element.17), channel_id=1, source_target_pairs={{0,4},{4,8},{8,12},{12,16},{16,20},{20,24},{24,28},{1,5},{5,9},{9,... | collective-permute-start | bytes 12296 | tf_op jit(solution)/shard_map/ppermute | solution.py:18
  6.3 1.3 collective-permute-start.1
  7.6 1.1 fusion.20
  8.7 4.5 %collective-permute-start.4 = (bf16[64,1,256]{2,1,0:T(2,128)(2,1)S(1)}, bf16[64,1,256]{2,1,0:T(2,128)(2,1)S(1)}, u32[]{:S(2)}, u32[]{:S(2)}) collective-permute-start(bf16[64,1,256]{2,1,0:T(2,128)(2,1)S(1)} %get-tuple-element.10), channel_id=1, source_target_pairs={{0,4},{4,8},{8,12},{12,16},{16,20},{20,24},{24,28},{1,5},{5,9},{9,... | collective-permute-start | bytes 98312 | tf_op jit(solution)/shard_map/ppermute | solution.py:40
  13.3 1.3 collective-permute-start.5
  14.6 1.0 pad_maximum_fusion.1
  15.7 1.3 collective-permute-start.2
  17.0 1.3 collective-permute-start.3
  18.3 2.0 %fusion.19 = (bf16[64,64,1]{2,1,0:T(8,128)(2,1)S(1)}, bf16[64,64,1]{2,1,0:T(8,128)(2,1)S(1)}) fusion(bf16[64,64,256]{2,1,0:T(8,128)(2,1)} %field.1), kind=kLoop, calls=%fused_computation.43 | loop fusion | bytes 32768 | tf_op jit(solution)/shard_map/slice | solution.py:32
  20.3 0.5 copy.49
  20.8 0.5 copy.50
  21.2 0.8 collective-permute-done.3
  22.0 0.2 pad_maximum_fusion
  22.7 0.2 fusion.14
  23.2 0.1 fusion.25
  23.3 0.5 copy.31
  23.8 0.1 fusion.26
  23.9 0.5 copy.32
  24.5 5.6 %collective-permute-start.6 = (bf16[64,66,1]{1,0,2:T(8,128)(2,1)S(1)}, bf16[64,66,1]{1,0,2:T(8,128)(2,1)S(1)}, u32[]{:S(2)}, u32[]{:S(2)}) collective-permute-start(bf16[64,66,1]{1,0,2:T(8,128)(2,1)S(1)} %pad_maximum_fusion.2), channel_id=1, source_target_pairs={{0,1},{1,2},{2,3},{4,5},{5,6},{6,7},{8,9},{9,10},{10,11},{12,13},{... | collective-permute-start | bytes 25352 | tf_op jit(solution)/shard_map/ppermute | solution.py:40
  30.1 0.5 copy.34
  30.6 0.5 copy.35
  31.2 1.3 collective-permute-start.7
  32.5 0.1 bitcast_dynamic-update-slice_fusion.planes
  32.6 0.6 copy.36.west
  33.2 1.1 collective-permute-done.7
  34.2 1.6 %copy.37.east = bf16[64,66,1]{2,1,0:T(8,128)(2,1)} copy(bf16[64,66,1]{1,0,2:T(8,128)(2,1)S(1)} %collective-permute-done.7) | data formatting | bytes 16896 | tf_op jit(solution)/shard_map/ppermute | solution.py:41
  35.8 1.6 %copy-done = bf16[64,64,256]{2,1,0:T(8,128)(2,1)S(1)} copy-done((bf16[64,64,256]{2,1,0:T(8,128)(2,1)S(1)}, bf16[64,64,256]{2,1,0:T(8,128)(2,1)}, u32[]{:S(2)}) %copy-start) | copy-done | bytes 2097176
  37.4 1.3 copy-done.3
  38.7 1.1 copy-done.5
  39.8 8.5 %shard_map.76.field = bf16[64,64,256]{2,1,0:T(8,128)(2,1)S(1)} custom-call(f32[9,64,256]{2,1,0:T(8,128)S(1)} %copy-done.5, bf16[64,64,256]{2,1,0:T(8,128)(2,1)S(1)} %copy-done, bf16[64,1,256]{2,1,0:T(2,128)(2,1)S(1)} %collective-permute-done.4.north, bf16[64,1,256]{2,1,0:T(2,128)(2,1)S(1)} %collective-permute-done.5.south, ...), custom_call_target="tpu_custom_call" | custom-call | tf_op jit(solution)/shard_map/pallas_call | solution.py:94
  48.3 0.1 fusion.18
  48.4 5.0 %collective-permute-start.8 = (bf16[64,1,256]{2,1,0:T(2,128)(2,1)S(1)}, bf16[64,1,256]{2,1,0:T(2,128)(2,1)S(1)}, u32[]{:S(2)}, u32[]{:S(2)}) collective-permute-start(bf16[64,1,256]{2,1,0:T(2,128)(2,1)S(1)} %get-tuple-element.6), channel_id=1, source_target_pairs={{0,4},{4,8},{8,12},{12,16},{16,20},{20,24},{24,28},{1,5},{5,9},{9,... | collective-permute-start | bytes 98312 | tf_op jit(solution)/shard_map/ppermute | solution.py:40
  53.4 1.5 fusion.17
  54.9 1.7 %copy.42 = bf16[64,64,1]{1,0,2:T(8,128)(2,1)S(1)} copy(bf16[64,64,1]{2,1,0:T(8,128)(2,1)} %get-tuple-element.3) | data formatting | bytes 16384 | tf_op jit(solution)/shard_map/slice | solution.py:32
  56.6 1.3 collective-permute-start.9
  57.9 0.5 copy.39
  58.3 0.1 fusion.23
  58.4 0.5 copy.41
  58.9 4.7 %collective-permute-done.9.south = bf16[64,1,256]{2,1,0:T(2,128)(2,1)S(1)} collective-permute-done((bf16[64,1,256]{2,1,0:T(2,128)(2,1)S(1)}, bf16[64,1,256]{2,1,0:T(2,128)(2,1)S(1)}, u32[]{:S(2)}, u32[]{:S(2)}) %collective-permute-start.9) | collective-permute-done | bytes 32800 | tf_op jit(solution)/shard_map/ppermute | solution.py:41
  63.6 0.1 fusion.24
  63.7 0.5 copy.43
  64.3 1.3 collective-permute-start.11
  65.6 0.5 copy.38
  66.1 0.5 copy.40
  66.7 3.7 %collective-permute-start.10 = (bf16[64,66,1]{1,0,2:T(8,128)(2,1)S(1)}, bf16[64,66,1]{1,0,2:T(8,128)(2,1)S(1)}, u32[]{:S(2)}, u32[]{:S(2)}) collective-permute-start(bf16[64,66,1]{1,0,2:T(8,128)(2,1)S(1)} %pad_maximum_fusion.4), channel_id=1, source_target_pairs={{0,1},{1,2},{2,3},{4,5},{5,6},{6,7},{8,9},{9,10},{10,11},{12,13},{... | collective-permute-start | bytes 25352 | tf_op jit(solution)/shard_map/ppermute | solution.py:40
  70.4 0.6 copy.45.east
  71.1 1.6 %copy.44.west = bf16[64,66,1]{2,1,0:T(8,128)(2,1)} copy(bf16[64,66,1]{1,0,2:T(8,128)(2,1)S(1)} %collective-permute-done.10) | data formatting | bytes 16896 | tf_op jit(solution)/shard_map/ppermute | solution.py:40
  72.7 1.3 copy-done.2
  73.9 1.1 copy-done.6
  75.0 9.4 %shard_map.77 = bf16[64,64,256]{2,1,0:T(8,128)(2,1)} custom-call(f32[9,64,256]{2,1,0:T(8,128)S(1)} %copy-done.6, bf16[64,64,256]{2,1,0:T(8,128)(2,1)S(1)} %shard_map.76.field, bf16[64,1,256]{2,1,0:T(2,128)(2,1)S(1)} %collective-permute-done.8.north, bf16[64,1,256]{2,1,0:T(2,128)(2,1)S(1)} %collective-permute-done.9.south, bf16[64,66,1]{2,1,0:T(8,128)(2,1)S(1)} %copy-done.2, ...), custom_call_target="tpu_custom_call" | custom-call | tf_op jit(solution)/shard_map/pallas_call | solution.py:94
  84.4 6.0 %fusion.3 = f32[64,64]{0,1:T(8,128)S(1)} fusion(bf16[64,64,256]{2,1,0:T(8,128)(2,1)S(1)} %copy-done.1, bf16[64,64,256]{2,1,0:T(8,128)(2,1)} %shard_map.77), kind=kOutput, calls=%fused_computation.3 | convolution fusion | flops 134217728 | bytes 4210688 | tf_op jit(solution)/shard_map/dot_general | solution.py:219
  90.5 0.1 broadcast_in_dim.2
  90.7 1.5 reshape.14
  92.1 8.4 %all-to-all-start = ((f32[32,1,4096]{2,1,0:T(1,128)}), f32[32,1,4096]{2,1,0:T(1,128)S(1)}, u32[]{:S(2)}, u32[]{:S(2)}) async-start(f32[32,1,4096]{2,1,0:T(1,128)} %reshape.14), calls=%async_computation | async-start | bytes 1048576 | tf_op jit(solution)/shard_map/all_to_all | solution.py:226
  100.6 4.4 %shard_map.78 = bf16[32,80,128]{2,1,0:T(8,128)(2,1)} custom-call(s32[32]{0:T(128)S(1)} %bitcast.33, bf16[64,3200]{1,0:T(8,128)(2,1)S(1)} %copy-done.7, s32[1,3200]{1,0:T(1,128)S(1)} %reshape.12.cells_ref), custom_call_target="tpu_custom_call" | custom-call | tf_op jit(solution)/shard_map/pallas_call | solution.py:138
  105.0 11.1 %all-to-all-done = f32[32,1,4096]{2,1,0:T(1,128)S(1)} async-done(((f32[32,1,4096]{2,1,0:T(1,128)}), f32[32,1,4096]{2,1,0:T(1,128)S(1)}, u32[]{:S(2)}, u32[]{:S(2)}) %all-to-all-start) | async-done | bytes 524320 | tf_op jit(solution)/shard_map/all_to_all | solution.py:226
  116.1 3.1 %all-to-all-start.1 = ((bf16[32,80,128]{2,1,0:T(8,128)(2,1)}), bf16[32,80,128]{2,1,0:T(8,128)(2,1)S(1)}, u32[]{:S(2)}, u32[]{:S(2)}) async-start(bf16[32,80,128]{2,1,0:T(8,128)(2,1)} %shard_map.78), calls=%async_computation.1 | async-start | bytes 1310720 | tf_op jit(solution)/shard_map/all_to_all | solution.py:231
  119.2 0.5 broadcast.34
  119.7 1.9 %reduce = f32[32,4096]{1,0:T(8,128)S(1)} reduce(f32[32,1,4096]{2,1,0:T(1,128)S(1)} %all-to-all-done, f32[]{:T(128)} %broadcast.34), dimensions={1}, to_apply=%all_to_all.6.reduce_sub_computation | reduce | bytes 1048580 | tf_op jit(solution)/shard_map/all_to_all | solution.py:226
  121.6 0.4 reshape.15
  122.1 0.6 broadcast_multiply_fusion
  122.7 14.4 %all-to-all-done.1.got_ref = bf16[32,80,128]{2,1,0:T(8,128)(2,1)S(1)} async-done(((bf16[32,80,128]{2,1,0:T(8,128)(2,1)}), bf16[32,80,128]{2,1,0:T(8,128)(2,1)S(1)}, u32[]{:S(2)}, u32[]{:S(2)}) %all-to-all-start.1) | async-done | bytes 655392 | tf_op jit(solution)/shard_map/all_to_all | solution.py:231
  137.1 18.8 %shard_map.79 = bf16[64,64,256]{2,1,0:T(8,128)(2,1)} custom-call(bf16[32,80,128]{2,1,0:T(8,128)(2,1)S(1)} %all-to-all-done.1.got_ref), custom_call_target="tpu_custom_call" | custom-call | tf_op jit(solution)/shard_map/pallas_call | solution.py:193
  (42 shorter events, 1.4 us)
Async XLA Ops:
  1.4 13.1 %collective-permute-start = (f32[4,1,256]{2,1,0:T(1,128)S(1)}, f32[4,1,256]{2,1,0:T(1,128)S(1)}, u32[]{:S(2)}, u32[]{:S(2)}) collective-permute-start(f32[4,1,256]{2,1,0:T(1,128)S(1)} %get-tuple-element.17), channel_id=1, source_target_pairs={{0,4},{4,8},{8,12},{12,16},{16,20},{20,24},{24,28},{1,5},{5,9},{9,... | collective-permute-start | bytes 12296 | tf_op jit(solution)/shard_map/ppermute | solution.py:18
  6.3 8.3 %collective-permute-start.1 = (f32[4,1,256]{2,1,0:T(1,128)S(1)}, f32[4,1,256]{2,1,0:T(1,128)S(1)}, u32[]{:S(2)}, u32[]{:S(2)}) collective-permute-start(f32[4,1,256]{2,1,0:T(1,128)S(1)} %get-tuple-element.18), channel_id=1, source_target_pairs={{4,0},{8,4},{12,8},{16,12},{20,16},{24,20},{28,24},{5,1},{9,5},{13... | collective-permute-start | bytes 12296 | tf_op jit(solution)/shard_map/ppermute | solution.py:21
  8.7 14.5 %collective-permute-start.4 = (bf16[64,1,256]{2,1,0:T(2,128)(2,1)S(1)}, bf16[64,1,256]{2,1,0:T(2,128)(2,1)S(1)}, u32[]{:S(2)}, u32[]{:S(2)}) collective-permute-start(bf16[64,1,256]{2,1,0:T(2,128)(2,1)S(1)} %get-tuple-element.10), channel_id=1, source_target_pairs={{0,4},{4,8},{8,12},{12,16},{16,20},{20,24},{24,28},{1,5},{5,9},{9,... | collective-permute-start | bytes 98312 | tf_op jit(solution)/shard_map/ppermute | solution.py:40
  13.3 10.5 %collective-permute-start.5 = (bf16[64,1,256]{2,1,0:T(2,128)(2,1)S(1)}, bf16[64,1,256]{2,1,0:T(2,128)(2,1)S(1)}, u32[]{:S(2)}, u32[]{:S(2)}) collective-permute-start(bf16[64,1,256]{2,1,0:T(2,128)(2,1)S(1)} %get-tuple-element.9), channel_id=1, source_target_pairs={{4,0},{8,4},{12,8},{16,12},{20,16},{24,20},{28,24},{5,1},{9,5},{13... | collective-permute-start | bytes 98312 | tf_op jit(solution)/shard_map/ppermute | solution.py:41
  15.7 5.6 %collective-permute-start.2 = (f32[4,66,1]{2,1,0:T(8,128)S(1)}, f32[4,66,1]{2,1,0:T(8,128)S(1)}, u32[]{:S(2)}, u32[]{:S(2)}) collective-permute-start(f32[4,66,1]{2,1,0:T(8,128)S(1)} %get-tuple-element.15), channel_id=1, source_target_pairs={{0,1},{1,2},{2,3},{4,5},{5,6},{6,7},{8,9},{9,10},{10,11},{12,13},{... | collective-permute-start | bytes 3176 | tf_op jit(solution)/shard_map/ppermute | solution.py:18
  17.0 5.0 %collective-permute-start.3 = (f32[4,66,1]{2,1,0:T(8,128)S(1)}, f32[4,66,1]{2,1,0:T(8,128)S(1)}, u32[]{:S(2)}, u32[]{:S(2)}) collective-permute-start(f32[4,66,1]{2,1,0:T(8,128)S(1)} %get-tuple-element.16), channel_id=1, source_target_pairs={{1,0},{2,1},{3,2},{5,4},{6,5},{7,6},{9,8},{10,9},{11,10},{13,12},{... | collective-permute-start | bytes 3176 | tf_op jit(solution)/shard_map/ppermute | solution.py:21
  20.3 1.7 %copy-start.9 = (f32[4,64,256]{2,1,0:T(8,128)S(1)}, f32[4,64,256]{2,1,0:T(8,128)}, u32[]{:S(2)}) copy-start(f32[4,64,256]{2,1,0:T(8,128)} %param.6) | copy-start | bytes 786436
  24.5 8.1 %collective-permute-start.6 = (bf16[64,66,1]{1,0,2:T(8,128)(2,1)S(1)}, bf16[64,66,1]{1,0,2:T(8,128)(2,1)S(1)}, u32[]{:S(2)}, u32[]{:S(2)}) collective-permute-start(bf16[64,66,1]{1,0,2:T(8,128)(2,1)S(1)} %pad_maximum_fusion.2), channel_id=1, source_target_pairs={{0,1},{1,2},{2,3},{4,5},{5,6},{6,7},{8,9},{9,10},{10,11},{12,13},{... | collective-permute-start | bytes 25352 | tf_op jit(solution)/shard_map/ppermute | solution.py:40
  31.2 3.1 %collective-permute-start.7 = (bf16[64,66,1]{1,0,2:T(8,128)(2,1)S(1)}, bf16[64,66,1]{1,0,2:T(8,128)(2,1)S(1)}, u32[]{:S(2)}, u32[]{:S(2)}) collective-permute-start(bf16[64,66,1]{1,0,2:T(8,128)(2,1)S(1)} %pad_maximum_fusion.3), channel_id=1, source_target_pairs={{1,0},{2,1},{3,2},{5,4},{6,5},{7,6},{9,8},{10,9},{11,10},{13,12},{... | collective-permute-start | bytes 25352 | tf_op jit(solution)/shard_map/ppermute | solution.py:41
  32.6 1.7 %copy-start.4 = (f32[9,64,256]{2,1,0:T(8,128)}, f32[9,64,256]{2,1,0:T(8,128)S(1)}, u32[]{:S(2)}) copy-start(f32[9,64,256]{2,1,0:T(8,128)S(1)} %bitcast_dynamic-update-slice_fusion.planes) | copy-start | bytes 1769476
  35.8 1.6 %copy-start = (bf16[64,64,256]{2,1,0:T(8,128)(2,1)S(1)}, bf16[64,64,256]{2,1,0:T(8,128)(2,1)}, u32[]{:S(2)}) copy-start(bf16[64,64,256]{2,1,0:T(8,128)(2,1)} %field.1) | copy-start | bytes 6291460
  37.4 1.3 copy-start.3
  38.7 1.1 copy-start.5
  48.4 10.0 %collective-permute-start.8 = (bf16[64,1,256]{2,1,0:T(2,128)(2,1)S(1)}, bf16[64,1,256]{2,1,0:T(2,128)(2,1)S(1)}, u32[]{:S(2)}, u32[]{:S(2)}) collective-permute-start(bf16[64,1,256]{2,1,0:T(2,128)(2,1)S(1)} %get-tuple-element.6), channel_id=1, source_target_pairs={{0,4},{4,8},{8,12},{12,16},{16,20},{20,24},{24,28},{1,5},{5,9},{9,... | collective-permute-start | bytes 98312 | tf_op jit(solution)/shard_map/ppermute | solution.py:40
  56.6 7.1 %collective-permute-start.9 = (bf16[64,1,256]{2,1,0:T(2,128)(2,1)S(1)}, bf16[64,1,256]{2,1,0:T(2,128)(2,1)S(1)}, u32[]{:S(2)}, u32[]{:S(2)}) collective-permute-start(bf16[64,1,256]{2,1,0:T(2,128)(2,1)S(1)} %get-tuple-element.5), channel_id=1, source_target_pairs={{4,0},{8,4},{12,8},{16,12},{20,16},{24,20},{28,24},{5,1},{9,5},{13... | collective-permute-start | bytes 98312 | tf_op jit(solution)/shard_map/ppermute | solution.py:41
  64.3 6.1 %collective-permute-start.11 = (bf16[64,66,1]{1,0,2:T(8,128)(2,1)S(1)}, bf16[64,66,1]{1,0,2:T(8,128)(2,1)S(1)}, u32[]{:S(2)}, u32[]{:S(2)}) collective-permute-start(bf16[64,66,1]{1,0,2:T(8,128)(2,1)S(1)} %pad_maximum_fusion.5), channel_id=1, source_target_pairs={{1,0},{2,1},{3,2},{5,4},{6,5},{7,6},{9,8},{10,9},{11,10},{13,12},{... | collective-permute-start | bytes 25352 | tf_op jit(solution)/shard_map/ppermute | solution.py:41
  66.7 4.4 %collective-permute-start.10 = (bf16[64,66,1]{1,0,2:T(8,128)(2,1)S(1)}, bf16[64,66,1]{1,0,2:T(8,128)(2,1)S(1)}, u32[]{:S(2)}, u32[]{:S(2)}) collective-permute-start(bf16[64,66,1]{1,0,2:T(8,128)(2,1)S(1)} %pad_maximum_fusion.4), channel_id=1, source_target_pairs={{0,1},{1,2},{2,3},{4,5},{5,6},{6,7},{8,9},{9,10},{10,11},{12,13},{... | collective-permute-start | bytes 25352 | tf_op jit(solution)/shard_map/ppermute | solution.py:40
  72.7 1.3 copy-start.2
  73.9 1.1 copy-start.6
  75.0 9.4 %copy-start.1 = (bf16[64,64,256]{2,1,0:T(8,128)(2,1)S(1)}, bf16[64,64,256]{2,1,0:T(8,128)(2,1)}, u32[]{:S(2)}) copy-start(bf16[64,64,256]{2,1,0:T(8,128)(2,1)} %field.1) | copy-start | bytes 6291460
  90.4 10.1 %copy-start.10 = (s32[3200]{0:T(1024)S(1)}, s32[3200]{0:T(1024)}, u32[]{:S(2)}) copy-start(s32[3200]{0:T(1024)} %param.8) | copy-start | bytes 38404
  90.4 10.1 %copy-start.7 = (bf16[64,3200]{1,0:T(8,128)(2,1)S(1)}, bf16[64,3200]{1,0:T(8,128)(2,1)}, u32[]{:S(2)}) copy-start(bf16[64,3200]{1,0:T(8,128)(2,1)} %rows_ref.1) | copy-start | bytes 1228804
  90.4 10.1 %copy-start.8 = (s32[1,32]{1,0:T(1,128)S(1)}, s32[1,32]{1,0:T(1,128)}, u32[]{:S(2)}) copy-start(s32[1,32]{1,0:T(1,128)} %param.9) | copy-start | bytes 388
  92.1 24.0 %all-to-all-start = ((f32[32,1,4096]{2,1,0:T(1,128)}), f32[32,1,4096]{2,1,0:T(1,128)S(1)}, u32[]{:S(2)}, u32[]{:S(2)}) async-start(f32[32,1,4096]{2,1,0:T(1,128)} %reshape.14), calls=%async_computation | async-start | bytes 1048576 | tf_op jit(solution)/shard_map/all_to_all | solution.py:226
  116.1 21.0 %all-to-all-start.1 = ((bf16[32,80,128]{2,1,0:T(8,128)(2,1)}), bf16[32,80,128]{2,1,0:T(8,128)(2,1)S(1)}, u32[]{:S(2)}, u32[]{:S(2)}) async-start(bf16[32,80,128]{2,1,0:T(8,128)(2,1)} %shard_map.78), calls=%async_computation.1 | async-start | bytes 1310720 | tf_op jit(solution)/shard_map/all_to_all | solution.py:231
